TPU v7x, 256 devices: a whole 4x4x8 slice. The times are simulated.
256 devices in a mesh: dp: 32 (over y, z), pipe: 8 (over x, core).
Axes of the slice: x: 4, y: 4, z: 8, core: 2. Of those that a mesh axis runs over, the one named last changes fastest.
Arguments:
- mel_tiles: bfloat16 [1024, 4, 320], P('dp'), may hold values from -6 to 6
- utt_ids: int32 [1024], P('dp'), may hold values from 0 to 2
- tile_lengths: int32 [1024], P('dp'), may hold values from 1 to 4, as said below
- dest_shard: int32 [1024], P('dp'), may hold values from 0 to 31, as said below
- dest_slot: int32 [1024], P('dp'), may hold values from 0 to 31, as said below
- subsample_weight: bfloat16 [320, 1536], replicated, may hold values from -0.3125 to 0.3125
- mixing_weight: bfloat16 [8, 1536, 1536], P('pipe', 'dp'), may hold values from -0.15625 to 0.15625
- gate_weight: bfloat16 [8, 1536, 1536], P('pipe', 'dp'), may hold values from -0.15625 to 0.15625
- conv_taps: float32 [8, 31, 1536], P('pipe'), may hold values from -1 to 1
- norm_gain: float32 [8, 1536], P('pipe'), may hold values from 0.5 to 1.5
- out_cot: bfloat16 [4096, 1536], P('dp'), may hold values from -0.09375 to 0.09375
Outputs:
- weight_grad: float32 [8, 1536, 1536], P('pipe', 'dp')
- gate_grad: float32 [8, 1536, 1536], P('pipe', 'dp')
- taps_grad: float32 [8, 31, 1536], P('pipe')
- gain_grad: float32 [8, 1536], P('pipe')
Inputs may be any that keep to these rules, and one draw needn't show every extreme that they name: `tile_lengths`: every loader shard's first tile has 4 live frames. `dest_shard`: each loader shard sends exactly 32 // 32 of its tiles to every data shard. `dest_slot`: the tiles that go to one data shard fill its slots, each slot once.
All inputs are finite; a program needn't handle non-finite values.
Results may differ from a plain program's by a relative error of at most 0.033.
Values may be sent and summed in bfloat16 or wider, within the bound.
A program may use at most 192 MiB of HBM per device.

v0:
```python
import jax
import jax.numpy as jnp
from jax import lax
from jax.sharding import PartitionSpec as P

MB = 2


EPSILON = 1e-05


def passed_along(value, axis, steps):
    count = lax.axis_size(axis)
    initial, last = (max(0, -steps), min(count, count - steps))
    return lax.ppermute(value, axis, [(source, source + steps) for source in range(initial, last)])


def normalize(inputs, gain):
    center = jnp.mean(inputs, axis=-1, keepdims=True)
    shifted = inputs - center
    spread = jnp.mean(shifted * shifted, axis=-1, keepdims=True)
    return shifted * lax.rsqrt(spread + EPSILON) * gain


def conv_sum(masked, taps, labels):
    reach = taps.shape[0] // 2
    length = masked.shape[0]
    padded = jnp.pad(masked, ((reach, reach), (0, 0)))
    padded_labels = jnp.pad(labels, ((reach, reach),), constant_values=-1)
    total = jnp.zeros(masked.shape, jnp.float32)
    for offset in range(taps.shape[0]):
        same = (padded_labels[offset : offset + length] == labels).astype(jnp.float32)
        total = total + taps[offset] * padded[offset : offset + length] * same[:, None]
    return total


def tap_terms(masked_all, spread_all, labels_all, count):
    reach = count // 2
    length = masked_all.shape[1]
    padded = jnp.pad(masked_all, ((0, 0), (reach, reach), (0, 0)))
    padded_labels = jnp.pad(labels_all, ((0, 0), (reach, reach)), constant_values=-1)
    terms = []
    for offset in range(count):
        same = (padded_labels[:, offset : offset + length] == labels_all).astype(jnp.float32)
        terms.append(
            jnp.sum(spread_all * padded[:, offset : offset + length] * same[..., None], axis=(0, 1))
        )
    return jnp.stack(terms, axis=0)


def body(
    mel_tiles,
    utt_ids,
    tile_lengths,
    dest_shard,
    dest_slot,
    subsample_weight,
    mixing_weight,
    gate_weight,
    conv_taps,
    norm_gain,
    out_cot,
):
    shards = lax.axis_size("dp")
    sections = lax.axis_size("pipe")
    position = lax.axis_index("pipe")
    tiles = mel_tiles.shape[0]
    frames_per_tile = mel_tiles.shape[1]
    features = mel_tiles.shape[2]
    width = subsample_weight.shape[1]
    per_peer = tiles // shards
    peers = jnp.arange(shards, dtype=jnp.int32)
    chosen = (dest_shard[:, None] == peers[None, :]).astype(jnp.int32)
    before = jnp.cumsum(chosen, axis=0) - chosen
    rank_in_peer = jnp.sum(before * chosen, axis=1)
    bucket = dest_shard * per_peer + rank_in_peer
    flat_tiles = mel_tiles.reshape(tiles, frames_per_tile * features)
    outgoing = jnp.zeros_like(flat_tiles).at[bucket].set(flat_tiles)
    details = jnp.stack([dest_slot, utt_ids, tile_lengths], axis=1)
    outgoing_details = jnp.zeros_like(details).at[bucket].set(details)
    arrived, arrived_details = (
        lax.all_to_all(outgoing, "dp", split_axis=0, concat_axis=0, tiled=True),
        lax.all_to_all(outgoing_details, "dp", split_axis=0, concat_axis=0, tiled=True),
    )
    slot_index = arrived_details[:, 0]
    placed = jnp.zeros_like(arrived).at[slot_index].set(arrived)
    slot_label = jnp.zeros((tiles,), jnp.int32).at[slot_index].set(arrived_details[:, 1])
    slot_length = jnp.zeros((tiles,), jnp.int32).at[slot_index].set(arrived_details[:, 2])
    frame_ids = jnp.arange(frames_per_tile, dtype=jnp.int32)
    frame_mask = (frame_ids[None, :] < slot_length[:, None]).astype(jnp.float32).reshape(MB, -1)
    labels = jnp.broadcast_to(slot_label[:, None], (tiles, frames_per_tile)).reshape(MB, -1)
    rows_mb = frame_mask.shape[1]
    embedded = jnp.dot(
        placed.reshape(tiles * frames_per_tile, features),
        subsample_weight,
        preferred_element_type=jnp.float32,
    )
    embedded = embedded.astype(jnp.bfloat16).reshape(MB, rows_mb, width)
    value_whole, gate_whole = (
        lax.all_gather(mixing_weight, "dp", axis=1, tiled=True),
        lax.all_gather(gate_weight, "dp", axis=1, tiled=True),
    )
    value_weight = value_whole[0]
    gating = gate_whole[0]
    taps = conv_taps[0]
    gain = norm_gain[0]
    tap_count = taps.shape[0]
    cot_blocks = out_cot.reshape(MB, rows_mb, width)
    ticks = MB + sections - 1

    def forward_section(source, micro):
        as_float = source.astype(jnp.float32)
        normed = normalize(as_float, gain).astype(jnp.bfloat16)
        value = jnp.dot(normed, value_weight, preferred_element_type=jnp.float32)
        gate = jnp.dot(normed, gating, preferred_element_type=jnp.float32)
        mask_row = frame_mask[micro]
        masked = value * jax.nn.sigmoid(gate) * mask_row[:, None]
        conv_out = conv_sum(masked, taps, labels[micro]) * mask_row[:, None]
        output = as_float + conv_out * jax.nn.sigmoid(conv_out)
        return (output.astype(jnp.bfloat16), value, gate)

    def forward_skip(source, micro):
        blank = jnp.zeros((rows_mb, width), jnp.float32)
        return (jnp.zeros_like(source), blank, blank)

    inbox = jnp.zeros((rows_mb, width), jnp.bfloat16)
    saved_inputs = jnp.zeros((MB + 1, rows_mb, width), jnp.bfloat16)
    saved_value = jnp.zeros((MB + 1, rows_mb, width), jnp.float32)
    saved_gate = jnp.zeros((MB + 1, rows_mb, width), jnp.float32)
    for tick in range(ticks):
        micro = tick - position
        valid = (micro >= 0) & (micro < MB)
        micro = jnp.clip(micro, 0, MB - 1)
        target = jnp.where(valid, micro, MB)
        source = jnp.where(position == 0, embedded[micro], inbox)
        result, value, gate = lax.cond(valid, forward_section, forward_skip, source, micro)
        saved_inputs = lax.dynamic_update_index_in_dim(saved_inputs, source, target, 0)
        saved_value = lax.dynamic_update_index_in_dim(saved_value, value, target, 0)
        saved_gate = lax.dynamic_update_index_in_dim(saved_gate, gate, target, 0)
        if tick + 1 < ticks:
            inbox = passed_along(result, "pipe", 1)

    def backward_section(seed, micro):
        as_float = saved_inputs[micro].astype(jnp.float32)
        normed = normalize(as_float, gain).astype(jnp.bfloat16)
        value = saved_value[micro]
        gate = saved_gate[micro]
        mask_col = frame_mask[micro][:, None]
        label_row = labels[micro]
        sig_gate = jax.nn.sigmoid(gate)
        masked = value * sig_gate * mask_col

        def conv_only(masked_in):
            return conv_sum(masked_in, taps, label_row)

        total, conv_back = jax.vjp(conv_only, masked)
        conv_out = total * mask_col
        sig_conv = jax.nn.sigmoid(conv_out)
        seed_float = seed.astype(jnp.float32)
        spread = seed_float * (sig_conv * (1.0 + conv_out * (1.0 - sig_conv))) * mask_col
        grad_masked = conv_back(spread)[0]
        grad_proj = grad_masked * mask_col
        grad_value = (grad_proj * sig_gate).astype(jnp.bfloat16)
        grad_gate = (grad_proj * value * sig_gate * (1.0 - sig_gate)).astype(jnp.bfloat16)
        grad_normed = lax.dot_general(
            grad_value, value_weight, (((1,), (1,)), ((), ())), preferred_element_type=jnp.float32
        )
        grad_normed = grad_normed + lax.dot_general(
            grad_gate, gating, (((1,), (1,)), ((), ())), preferred_element_type=jnp.float32
        )
        _, norm_back = jax.vjp(normalize, as_float, gain)
        grad_input, grad_gain = norm_back(grad_normed)
        passed = (seed_float + grad_input).astype(jnp.bfloat16)
        grads_both = jnp.concatenate([grad_value, grad_gate], axis=1)
        return (passed, grad_gain, normed, grads_both, masked, spread)

    def backward_skip(seed, micro):
        blank = jnp.zeros((rows_mb, width), jnp.bfloat16)
        blank_both = jnp.zeros((rows_mb, 2 * width), jnp.bfloat16)
        blank_float = jnp.zeros((rows_mb, width), jnp.float32)
        return (
            jnp.zeros_like(seed),
            jnp.zeros_like(gain),
            blank,
            blank_both,
            blank_float,
            blank_float,
        )

    inbox = jnp.zeros((rows_mb, width), jnp.bfloat16)
    gain_total = jnp.zeros_like(gain)
    saved_normed = jnp.zeros((MB + 1, rows_mb, width), jnp.bfloat16)
    saved_grads = jnp.zeros((MB + 1, rows_mb, 2 * width), jnp.bfloat16)
    saved_masked = jnp.zeros((MB + 1, rows_mb, width), jnp.float32)
    saved_spread = jnp.zeros((MB + 1, rows_mb, width), jnp.float32)
    for tick in range(ticks):
        micro = tick - (sections - 1 - position)
        valid = (micro >= 0) & (micro < MB)
        micro = jnp.clip(micro, 0, MB - 1)
        target = jnp.where(valid, micro, MB)
        seed = jnp.where(position == sections - 1, cot_blocks[micro], inbox)
        passed, grad_gain, normed, grads_both, masked, spread = lax.cond(
            valid, backward_section, backward_skip, seed, micro
        )
        gain_total = gain_total + grad_gain
        saved_normed = lax.dynamic_update_index_in_dim(saved_normed, normed, target, 0)
        saved_grads = lax.dynamic_update_index_in_dim(saved_grads, grads_both, target, 0)
        saved_masked = lax.dynamic_update_index_in_dim(saved_masked, masked, target, 0)
        saved_spread = lax.dynamic_update_index_in_dim(saved_spread, spread, target, 0)
        if tick + 1 < ticks:
            inbox = passed_along(passed, "pipe", -1)
    tap_total = tap_terms(saved_masked[:MB], saved_spread[:MB], labels, tap_count)
    all_normed = saved_normed[:MB].reshape(MB * rows_mb, width)
    all_grads = saved_grads[:MB].reshape(MB * rows_mb, 2 * width)
    weight_rows = lax.psum_scatter(
        lax.dot_general(
            all_normed, all_grads, (((0,), (0,)), ((), ())), preferred_element_type=jnp.float32
        ).astype(jnp.bfloat16),
        "dp",
        scatter_dimension=0,
        tiled=True,
    ).astype(jnp.float32)
    tap_sum, gain_sum = (
        lax.psum(tap_total.astype(jnp.bfloat16), "dp").astype(jnp.float32),
        lax.psum(gain_total.astype(jnp.bfloat16), "dp").astype(jnp.float32),
    )
    return (
        weight_rows[:, :width][None],
        weight_rows[:, width:][None],
        tap_sum[None],
        gain_sum[None],
    )


def solution(mesh):
    in_specs = (
        P("dp", None, None),
        P("dp"),
        P("dp"),
        P("dp"),
        P("dp"),
        P(),
        P("pipe", "dp", None),
        P("pipe", "dp", None),
        P("pipe", None, None),
        P("pipe", None),
        P("dp", None),
    )
    out_specs = (
        P("pipe", "dp", None),
        P("pipe", "dp", None),
        P("pipe", None, None),
        P("pipe", None),
    )
    return jax.shard_map(body, mesh=mesh, in_specs=in_specs, out_specs=out_specs, check_vma=False)
```

profile of v0, /device:TPU:8, one launch (start us, length us, event | category | flops | bytes accessed | tf_op | source)
XLA Modules:
  0.0 1033.4 jit_solution(8933944776115927521)
XLA Ops:
  13.0 11.7 %all-to-all-start = ((s32[32,1,3]{2,1,0:T(1,128)}), s32[32,1,3]{2,1,0:T(1,128)S(1)}, u32[]{:S(2)}, u32[]{:S(2)}) async-start(s32[32,1,3]{2,1,0:T(1,128)} %bitcast.139), calls=%async_computation | async-start | bytes 32768 | tf_op jit(solution)/shard_map/all_to_all | solution.py:83
  28.7 4.6 all-to-all-done
  33.3 5.2 all-to-all-start.1
  43.3 4.3 all-to-all-done.1
  49.8 46.7 %all-gather.3.cloned.1.call-done = bf16[1,1536,1536]{2,1,0:T(8,128)(2,1)} async-done(((bf16[1,48,1536]{2,1,0:T(8,128)(2,1)}), bf16[1,1536,1536]{2,1,0:T(8,128)(2,1)}) %all-gather.3.cloned.1.call-update) | async-done | bytes 4718608 | tf_op jit(solution)/shard_map/all_gather | solution.py:100
  96.4 83.4 %all-gather.5.cloned.1.call-done = bf16[1,1536,1536]{2,1,0:T(8,128)(2,1)} async-done(((bf16[1,48,1536]{2,1,0:T(8,128)(2,1)}), bf16[1,1536,1536]{2,1,0:T(8,128)(2,1)}) %all-gather.5.cloned.1.call-update) | async-done | bytes 4718608 | tf_op jit(solution)/shard_map/all_gather | solution.py:101
  180.5 9.5 conditional.18
  181.4 3.5 fusion.97
  186.6 3.3 fusion.5
  193.3 17.8 %conditional.19 = (bf16[64,1536]{1,0:T(8,128)(2,1)}, f32[1,64,1536]{2,1,0:T(8,128)}, f32[1,64,1536]{2,1,0:T(8,128)}) conditional(s32[]{:T(128)} %convert_element_type.2713, () %tuple.299, (bf16[64,1536]{1,0:T(8,128)(2,1)}, f32[31,1536]{1,0:T(8,128)S(1)}, f32[1,1536]{1,0:T(1,128)S(1)}, bf16[1536,1536]{1,0:T(8,128)(2,1)}, ...), branch_computations={%region_11.12_spmd, %region_12.15_spmd} | conditional | flops 615780160 | bytes 32896310 | solution.py:136
  199.4 4.3 fusion.198
  204.1 2.7 multiply_multiply_fusion.1
  207.7 3.4 fusion.106
  211.1 2.3 collective-permute-start.1
  215.3 2.5 conditional.20
  217.8 19.1 %collective-permute-start.2 = (bf16[64,1536]{1,0:T(8,128)(2,1)}, bf16[64,1536]{1,0:T(8,128)(2,1)S(1)}, u32[]{:S(2)}, u32[]{:S(2)}) collective-permute-start(bf16[64,1536]{1,0:T(8,128)(2,1)} %get-tuple-element.1255), channel_id=1, source_target_pairs={{0,1},{1,2},{2,3},{3,4},{4,5},{5,6},{6,7},{8,9},{9,10},{10,11},{11... | collective-permute-start | bytes 589832 | tf_op jit(solution)/shard_map/ppermute | solution.py:15
  239.8 2.3 conditional.21
  242.0 5.1 collective-permute-start.3
  250.0 2.7 conditional.22
  252.6 20.6 %collective-permute-start.4 = (bf16[64,1536]{1,0:T(8,128)(2,1)}, bf16[64,1536]{1,0:T(8,128)(2,1)S(1)}, u32[]{:S(2)}, u32[]{:S(2)}) collective-permute-start(bf16[64,1536]{1,0:T(8,128)(2,1)} %get-tuple-element.1259), channel_id=1, source_target_pairs={{0,1},{1,2},{2,3},{3,4},{4,5},{5,6},{6,7},{8,9},{9,10},{10,11},{11... | collective-permute-start | bytes 589832 | tf_op jit(solution)/shard_map/ppermute | solution.py:15
  276.1 2.3 conditional.23
  278.4 5.1 collective-permute-start.5
  286.3 2.4 conditional.24
  288.7 13.8 %collective-permute-start.6 = (bf16[64,1536]{1,0:T(8,128)(2,1)}, bf16[64,1536]{1,0:T(8,128)(2,1)S(1)}, u32[]{:S(2)}, u32[]{:S(2)}) collective-permute-start(bf16[64,1536]{1,0:T(8,128)(2,1)} %get-tuple-element.1263), channel_id=1, source_target_pairs={{0,1},{1,2},{2,3},{3,4},{4,5},{5,6},{6,7},{8,9},{9,10},{10,11},{11... | collective-permute-start | bytes 589832 | tf_op jit(solution)/shard_map/ppermute | solution.py:15
  305.3 2.3 conditional.25
  307.6 5.1 collective-permute-start.7
  318.5 4.5 conditional.27
  328.5 1.8 constant_dynamic-update-slice_fusion.17
  332.7 9.9 collective-permute-done.8
  342.7 1.8 conditional.28
  346.6 1.8 constant_dynamic-update-slice_fusion.16
  349.9 5.7 collective-permute-done.9
  355.6 4.8 conditional.29
  363.5 1.8 constant_dynamic-update-slice_fusion.15
  368.7 3.7 collective-permute-done.10
  372.3 4.5 conditional.30
  379.9 1.8 constant_dynamic-update-slice_fusion.14
  385.1 2.8 collective-permute-done.11
  387.9 4.5 conditional.31
  395.5 1.8 constant_dynamic-update-slice_fusion.13
  400.7 8.1 collective-permute-done.12
  408.8 4.5 conditional.32
  416.4 1.8 constant_dynamic-update-slice_fusion.12
  421.6 2.8 collective-permute-done.13
  424.5 4.8 conditional.33
  432.3 1.8 constant_dynamic-update-slice_fusion.11
  437.5 139.6 %collective-permute-done.14 = bf16[64,1536]{1,0:T(8,128)(2,1)} collective-permute-done((bf16[64,1536]{1,0:T(8,128)(2,1)}, bf16[64,1536]{1,0:T(8,128)(2,1)}, u32[]{:S(2)}, u32[]{:S(2)}) %collective-permute-start.14) | collective-permute-done | bytes 196640 | tf_op jit(solution)/shard_map/ppermute | solution.py:15
  577.1 25.5 %conditional.34 = (bf16[64,1536]{1,0:T(8,128)(2,1)}, f32[1536]{0:T(1024)}, bf16[1,64,1536]{2,1,0:T(8,128)(2,1)}, bf16[1,64,3072]{2,1,0:T(8,128)(2,1)}, f32[1,64,1536]{2,1,0:T(8,128)}, /*index=5*/f32[1,64,1536]{2,1,0:T(8,128)}) conditional(s32[]{:T(128)} %convert_element_type.2727, () %tuple.328, (pred[]{:T(512)}, ...), branch_computations={%region_92.93_spmd, %region_93.99_spmd} | conditional | flops 631040576 | bytes 76348256 | solution.py:202
  582.4 4.3 multiply_multiply_fusion.262
  599.9 1.8 fusion.1614
  603.9 1.8 constant_dynamic-update-slice_fusion.1
  611.9 23.1 %conditional.35 = (f32[1536]{0:T(1024)}, bf16[1,64,1536]{2,1,0:T(8,128)(2,1)}, bf16[1,64,3072]{2,1,0:T(8,128)(2,1)S(1)}, f32[1,64,1536]{2,1,0:T(8,128)}, f32[1,64,1536]{2,1,0:T(8,128)}) conditional(s32[]{:T(128)} %convert_element_type.2728, () %tuple.330, (s32[]{:T(128)}, bf16[3,64,1536]{2,1,0:T(8,128)(2,1)S(1)}, f32[31,1536]{1,0:T(8,128)S(1)}, ...), branch_computations={%region_99.100_spmd, %region_100.104_spmd} | conditional | flops 628975936 | bytes 74360904 | solution.py:202
  617.3 4.3 multiply_multiply_fusion.294
  632.6 2.2 fusion.1728
  640.6 2.4 fusion.1914
  643.2 2.1 fusion.1917
  645.5 2.1 fusion.1920
  647.8 2.1 fusion.1923
  650.0 2.1 fusion.1911
  654.5 5.1 bitcast_convert_fusion
  661.2 64.5 %psum.15 = bf16[1,1536]{1,0:T(2,128)(2,1)S(1)} all-reduce(bf16[1,1536]{1,0:T(2,128)(2,1)S(1)} %broadcast_in_dim.947), channel_id=1, replica_groups=mesh['dp'=32,'pipe'=8] {'dp'}, use_global_device_ids=true, to_apply=%region_137.138 | all-reduce | flops 1536 | bytes 6144 | tf_op jit(solution)/shard_map/psum | solution.py:225
  726.3 64.6 %all-reduce.317.cloned.1.call-done = bf16[1,31,1536]{2,0,1:T(2,128)(2,1)} async-done(((bf16[1,31,1536]{2,0,1:T(2,128)(2,1)}), bf16[1,31,1536]{2,0,1:T(2,128)(2,1)}) %all-reduce.317.cloned.1.call-update) | async-done | bytes 95248 | tf_op jit(solution)/shard_map/psum | solution.py:224
  790.9 1.8 broadcast_in_dim.946
  792.7 231.9 %reduce-scatter.2.cloned.1.call-done = bf16[48,3072]{1,0:T(8,128)(2,1)} async-done(((bf16[1536,3072]{1,0:T(8,128)(2,1)}), bf16[48,3072]{1,0:T(8,128)(2,1)}) %reduce-scatter.2.cloned.1.call-update) | async-done | bytes 294928 | tf_op jit(solution)/shard_map/reduce_scatter | solution.py:215
  (677 shorter events, 191.2 us)
Async XLA Ops:
  7.2 41.4 %copy-start = (bf16[320,1536]{1,0:T(8,128)(2,1)S(1)}, bf16[320,1536]{1,0:T(8,128)(2,1)}, u32[]{:S(2)}) copy-start(bf16[320,1536]{1,0:T(8,128)(2,1)} %param.52) | copy-start | bytes 2949124
  7.2 21.5 %copy-start.33 = (f32[1,31,1536]{2,0,1:T(1,128)S(1)}, f32[1,31,1536]{2,0,1:T(1,128)}, u32[]{:S(2)}) copy-start(f32[1,31,1536]{2,0,1:T(1,128)} %param.55) | copy-start | bytes 571396
  7.2 89.2 %all-gather.3.cloned.1.call-start = ((), (), s32[]{:S(2)}) async-start(), calls=%async_computation.3 | async-start | bytes 4866048 | tf_op jit(solution)/shard_map/all_gather | solution.py:100
  7.9 171.9 %all-gather.5.cloned.1.call-start = ((), (), s32[]{:S(2)}) async-start(), calls=%async_computation.4 | async-start | bytes 4866048 | tf_op jit(solution)/shard_map/all_gather | solution.py:101
  13.0 20.3 %all-to-all-start = ((s32[32,1,3]{2,1,0:T(1,128)}), s32[32,1,3]{2,1,0:T(1,128)S(1)}, u32[]{:S(2)}, u32[]{:S(2)}) async-start(s32[32,1,3]{2,1,0:T(1,128)} %bitcast.139), calls=%async_computation | async-start | bytes 32768 | tf_op jit(solution)/shard_map/all_to_all | solution.py:83
  33.3 14.3 %all-to-all-start.1 = ((bf16[32,2,640]{2,1,0:T(2,128)(2,1)}), bf16[32,2,640]{2,1,0:T(2,128)(2,1)S(1)}, u32[]{:S(2)}, u32[]{:S(2)}) async-start(bf16[32,2,640]{2,1,0:T(2,128)(2,1)} %reshape.1815), calls=%async_computation.1 | async-start | bytes 163840 | tf_op jit(solution)/shard_map/all_to_all | solution.py:82
  38.5 752.4 %all-reduce.317.cloned.1.call-start = ((), (), s32[]{:S(2)}) async-start(), calls=%async_computation.6 | async-start | bytes 380928 | tf_op jit(solution)/shard_map/psum | solution.py:224
  40.4 152.9 %copy-start.36 = (s32[2,64]{1,0:T(2,128)}, s32[2,64]{1,0:T(2,128)S(1)}, u32[]{:S(2)}) copy-start(s32[2,64]{1,0:T(2,128)S(1)} %broadcast_in_dim.933) | copy-start | bytes 1540
  43.3 150.0 %copy-start.599 = (f32[2,64]{1,0:T(2,128)}, f32[2,64]{1,0:T(2,128)S(1)}, u32[]{:S(2)}) copy-start(f32[2,64]{1,0:T(2,128)S(1)} %compare_convert_fusion.540) | copy-start | bytes 1540
  48.6 131.9 %copy-start.29 = (f32[1,1536]{1,0:T(1,128)S(1)}, f32[1,1536]{1,0:T(1,128)}, u32[]{:S(2)}) copy-start(f32[1,1536]{1,0:T(1,128)} %param.56) | copy-start | bytes 18436
  181.4 3.8 copy-start.2
  190.0 2.5 collective-permute-start
  194.9 4.4 copy-start.322
  199.4 4.4 copy-start.3
  199.4 4.4 copy-start.14
  199.4 4.4 copy-start.323
  199.4 4.4 copy-start.585
  199.4 4.4 copy-start.592
  203.8 3.6 copy-start.366
  203.8 3.6 copy-start.367
  203.8 3.6 copy-start.368
  203.9 3.6 copy-start.369
  203.9 3.6 copy-start.370
  203.9 3.6 copy-start.371
  203.9 3.6 copy-start.372
  203.9 3.6 copy-start.373
  211.1 3.5 collective-permute-start.1
  217.8 21.2 %collective-permute-start.2 = (bf16[64,1536]{1,0:T(8,128)(2,1)}, bf16[64,1536]{1,0:T(8,128)(2,1)S(1)}, u32[]{:S(2)}, u32[]{:S(2)}) collective-permute-start(bf16[64,1536]{1,0:T(8,128)(2,1)} %get-tuple-element.1255), channel_id=1, source_target_pairs={{0,1},{1,2},{2,3},{3,4},{4,5},{5,6},{6,7},{8,9},{9,10},{10,11},{11... | collective-permute-start | bytes 589832 | tf_op jit(solution)/shard_map/ppermute | solution.py:15
  242.0 7.2 collective-permute-start.3
  252.6 22.7 %collective-permute-start.4 = (bf16[64,1536]{1,0:T(8,128)(2,1)}, bf16[64,1536]{1,0:T(8,128)(2,1)S(1)}, u32[]{:S(2)}, u32[]{:S(2)}) collective-permute-start(bf16[64,1536]{1,0:T(8,128)(2,1)} %get-tuple-element.1259), channel_id=1, source_target_pairs={{0,1},{1,2},{2,3},{3,4},{4,5},{5,6},{6,7},{8,9},{9,10},{10,11},{11... | collective-permute-start | bytes 589832 | tf_op jit(solution)/shard_map/ppermute | solution.py:15
  278.4 7.2 collective-permute-start.5
  288.7 15.9 %collective-permute-start.6 = (bf16[64,1536]{1,0:T(8,128)(2,1)}, bf16[64,1536]{1,0:T(8,128)(2,1)S(1)}, u32[]{:S(2)}, u32[]{:S(2)}) collective-permute-start(bf16[64,1536]{1,0:T(8,128)(2,1)} %get-tuple-element.1263), channel_id=1, source_target_pairs={{0,1},{1,2},{2,3},{3,4},{4,5},{5,6},{6,7},{8,9},{9,10},{10,11},{11... | collective-permute-start | bytes 589832 | tf_op jit(solution)/shard_map/ppermute | solution.py:15
  307.6 7.2 collective-permute-start.7
  323.1 19.6 %collective-permute-start.8 = (bf16[64,1536]{1,0:T(8,128)(2,1)}, bf16[64,1536]{1,0:T(8,128)(2,1)}, u32[]{:S(2)}, u32[]{:S(2)}) collective-permute-start(bf16[64,1536]{1,0:T(8,128)(2,1)} %get-tuple-element.1277), channel_id=1, source_target_pairs={{1,0},{2,1},{3,2},{4,3},{5,4},{6,5},{7,6},{9,8},{10,9},{11,10},{12... | collective-permute-start | bytes 589832 | tf_op jit(solution)/shard_map/ppermute | solution.py:15
  330.4 12.2 %copy-start.44 = (s32[2,64]{1,0:T(2,128)S(1)}, s32[2,64]{1,0:T(2,128)}, u32[]{:S(2)}) copy-start(s32[2,64]{1,0:T(2,128)} %copy-done.36) | copy-start | bytes 1540
  330.4 12.2 %copy-start.607 = (f32[2,64]{1,0:T(2,128)S(1)}, f32[2,64]{1,0:T(2,128)}, u32[]{:S(2)}) copy-start(f32[2,64]{1,0:T(2,128)} %copy-done.599) | copy-start | bytes 1540
  331.5 11.2 %copy-start.25 = (bf16[3,64,3072]{2,1,0:T(8,128)(2,1)}, bf16[3,64,3072]{2,1,0:T(8,128)(2,1)S(1)}, u32[]{:S(2)}) copy-start(bf16[3,64,3072]{2,1,0:T(8,128)(2,1)S(1)} %constant_dynamic-update-slice_fusion.26) | copy-start | bytes 3538948
  332.7 9.9 copy-start.27
  344.5 4.7 copy-start.34
  344.5 11.1 %collective-permute-start.9 = (bf16[64,1536]{1,0:T(8,128)(2,1)}, bf16[64,1536]{1,0:T(8,128)(2,1)}, u32[]{:S(2)}, u32[]{:S(2)}) collective-permute-start(bf16[64,1536]{1,0:T(8,128)(2,1)} %get-tuple-element.1279), channel_id=1, source_target_pairs={{1,0},{2,1},{3,2},{4,3},{5,4},{6,5},{7,6},{9,8},{10,9},{11,10},{12... | collective-permute-start | bytes 589832 | tf_op jit(solution)/shard_map/ppermute | solution.py:15
  346.6 9.0 copy-start.45
  346.6 9.0 copy-start.608
  360.4 11.9 %collective-permute-start.10 = (bf16[64,1536]{1,0:T(8,128)(2,1)}, bf16[64,1536]{1,0:T(8,128)(2,1)}, u32[]{:S(2)}, u32[]{:S(2)}) collective-permute-start(bf16[64,1536]{1,0:T(8,128)(2,1)} %get-tuple-element.1281), channel_id=1, source_target_pairs={{1,0},{2,1},{3,2},{4,3},{5,4},{6,5},{7,6},{9,8},{10,9},{11,10},{12... | collective-permute-start | bytes 589832 | tf_op jit(solution)/shard_map/ppermute | solution.py:15
  363.5 8.9 copy-start.46
  363.5 8.9 copy-start.609
  376.8 11.1 %collective-permute-start.11 = (bf16[64,1536]{1,0:T(8,128)(2,1)}, bf16[64,1536]{1,0:T(8,128)(2,1)}, u32[]{:S(2)}, u32[]{:S(2)}) collective-permute-start(bf16[64,1536]{1,0:T(8,128)(2,1)} %get-tuple-element.1283), channel_id=1, source_target_pairs={{1,0},{2,1},{3,2},{4,3},{5,4},{6,5},{7,6},{9,8},{10,9},{11,10},{12... | collective-permute-start | bytes 589832 | tf_op jit(solution)/shard_map/ppermute | solution.py:15
  379.9 8.0 copy-start.47
  379.9 8.0 copy-start.610
  392.4 16.4 %collective-permute-start.12 = (bf16[64,1536]{1,0:T(8,128)(2,1)}, bf16[64,1536]{1,0:T(8,128)(2,1)}, u32[]{:S(2)}, u32[]{:S(2)}) collective-permute-start(bf16[64,1536]{1,0:T(8,128)(2,1)} %get-tuple-element.1285), channel_id=1, source_target_pairs={{1,0},{2,1},{3,2},{4,3},{5,4},{6,5},{7,6},{9,8},{10,9},{11,10},{12... | collective-permute-start | bytes 589832 | tf_op jit(solution)/shard_map/ppermute | solution.py:15
  395.5 13.3 %copy-start.48 = (s32[2,64]{1,0:T(2,128)S(1)}, s32[2,64]{1,0:T(2,128)}, u32[]{:S(2)}) copy-start(s32[2,64]{1,0:T(2,128)} %copy-done.36) | copy-start | bytes 1540
  395.5 13.3 %copy-start.611 = (f32[2,64]{1,0:T(2,128)S(1)}, f32[2,64]{1,0:T(2,128)}, u32[]{:S(2)}) copy-start(f32[2,64]{1,0:T(2,128)} %copy-done.599) | copy-start | bytes 1540
  413.4 11.1 %collective-permute-start.13 = (bf16[64,1536]{1,0:T(8,128)(2,1)}, bf16[64,1536]{1,0:T(8,128)(2,1)}, u32[]{:S(2)}, u32[]{:S(2)}) collective-permute-start(bf16[64,1536]{1,0:T(8,128)(2,1)} %get-tuple-element.1287), channel_id=1, source_target_pairs={{1,0},{2,1},{3,2},{4,3},{5,4},{6,5},{7,6},{9,8},{10,9},{11,10},{12... | collective-permute-start | bytes 589832 | tf_op jit(solution)/shard_map/ppermute | solution.py:15
  416.4 8.0 copy-start.49
  416.4 8.0 copy-start.612
  429.2 147.8 %collective-permute-start.14 = (bf16[64,1536]{1,0:T(8,128)(2,1)}, bf16[64,1536]{1,0:T(8,128)(2,1)}, u32[]{:S(2)}, u32[]{:S(2)}) collective-permute-start(bf16[64,1536]{1,0:T(8,128)(2,1)} %get-tuple-element.1289), channel_id=1, source_target_pairs={{1,0},{2,1},{3,2},{4,3},{5,4},{6,5},{7,6},{9,8},{10,9},{11,10},{12... | collective-permute-start | bytes 589832 | tf_op jit(solution)/shard_map/ppermute | solution.py:15
  432.3 144.8 %copy-start.50 = (s32[2,64]{1,0:T(2,128)S(1)}, s32[2,64]{1,0:T(2,128)}, u32[]{:S(2)}) copy-start(s32[2,64]{1,0:T(2,128)} %copy-done.36) | copy-start | bytes 1540
  432.3 144.8 %copy-start.613 = (f32[2,64]{1,0:T(2,128)S(1)}, f32[2,64]{1,0:T(2,128)}, u32[]{:S(2)}) copy-start(f32[2,64]{1,0:T(2,128)} %copy-done.599) | copy-start | bytes 1540
  602.6 9.3 collective-permute-start.15
  605.7 6.3 copy-start.51
  605.7 6.3 copy-start.614
  650.0 4.5 copy-start.26
  650.0 4.5 copy-start.32
  653.4 371.1 %reduce-scatter.2.cloned.1.call-start = ((), (), s32[]{:S(2)}) async-start(), calls=%async_computation.5 | async-start | bytes 9732096 | tf_op jit(solution)/shard_map/reduce_scatter | solution.py:215
  725.7 300.7 %copy-start.1 = (bf16[320,1536]{1,0:T(8,128)(2,1)S(1)}, bf16[320,1536]{1,0:T(8,128)(2,1)}, u32[]{:S(2)}) copy-start(bf16[320,1536]{1,0:T(8,128)(2,1)} %param.52) | copy-start | bytes 2949124
  (144 other events, 324.9 us)
Sparse Core Ops, SparseCore 0:
  10.6 85.7 all-gather.2
  99.0 80.7 all-gather.4
  653.5 137.3 all-reduce.316
  795.3 229.1 reduce-scatter.1
where the time goes:
time: 1050 us; the launch traced here: 1030 us
  waiting for transfers between devices  611 us (58%)
  local copies, waits for them, and re-layouts  136 us (13%)
  starting transfers between devices  99.7 us (9%)
  other arithmetic  76.9 us (7%)
  blocking collectives  64.5 us (6%)
  matrix products  23.9 us (2%)
  between operations  16 us (2%)
    reduce_scatter x1, waiting for transfers between devices, body(): lax.psum_scatter(lax.dot_general(all_normed, all_grads, (((0,), (0,)), ((...  232 us
    ppermute x16, waiting for transfers between devices, passed_along(): lax.ppermute(value, axis, [(source, source + steps) for source in range(i...  174 us
    all_gather x1, waiting for transfers between devices, body(): lax.all_gather(gate_weight, 'dp', axis=1, tiled=True)  83.4 us
    ppermute x16, starting transfers between devices, passed_along(): lax.ppermute(value, axis, [(source, source + steps) for source in range(i...  82.6 us
    psum x1, waiting for transfers between devices, body(): lax.psum(tap_total.astype(jnp.bfloat16), 'dp').astype(jnp.float32)  64.6 us
    psum x1, blocking collectives, body(): lax.psum(gain_total.astype(jnp.bfloat16), 'dp').astype(jnp.float32)  64.5 us
    all_gather x1, waiting for transfers between devices, body(): lax.all_gather(mixing_weight, 'dp', axis=1, tiled=True)  46.7 us
  transfers between devices with their start and end apart: 22, of which 15 were waited for; matrix products, arithmetic and copies ran while one was open for 9% of the time, Pallas kernels for 0%

commit v1 on v0

v1 whole, which is shorter than its diff:
```python
import functools

import jax
import jax.numpy as jnp
from jax import lax
from jax.experimental import pallas as pl
from jax.experimental.pallas import tpu as pltpu
from jax.sharding import PartitionSpec as P

PHYS = {32: (4, 8), 8: (2, 4), 4: (2, 2)}
CORES = 2
EPSILON = 1e-05
F32 = jnp.float32
BF16 = jnp.bfloat16
VMEM_LIMIT = 60 * 1024 * 1024


def rcopy(src, dst, send_sem, recv_sem, device):
    return pltpu.make_async_remote_copy(
        src_ref=src,
        dst_ref=dst,
        send_sem=send_sem,
        recv_sem=recv_sem,
        device_id=device,
        device_id_type=pl.DeviceIdType.MESH,
    )


def kernel(
    dims,
    slabs,
    mixing,
    gating,
    tg,
    gain8,
    sub,
    cot,
    o_mix,
    o_gate,
    o_taps,
    W,
    TAPS,
    GAIN,
    T1,
    T2,
    TF,
    EA,
    CP,
    MASK,
    X,
    NT,
    NS,
    GL,
    SP,
    V,
    SG,
    CV,
    GC,
    PF,
    GO,
    GS,
    MS,
    MR,
    G,
    RA,
    RB,
    FS,
    FR,
    TT,
    TS,
    TY,
    TYR,
    TZR,
    TX,
    TXR,
    TO1,
    TO2,
    lw_s,
    xw_s,
    xw_r,
    tg_s,
    tg_r,
    tl_s,
    tl_r,
    ag_s,
    ag_r,
    rs_s,
    rs_r,
    sw_s,
    sw_r,
    st_s,
    st_r,
    xf_s,
    xf_r,
    xb_s,
    xb_r,
    sn_s,
    sn_r,
    sg_s,
    sg_r,
    fin_s,
    fin_r,
    tt_s,
    tt_r,
):
    NX, NY, NZ = dims["X"], dims["Y"], dims["Z"]
    D, R, FRM, TSUB, J, KT = (dims[k] for k in ("D", "R", "F", "TSUB", "J", "TAPS"))
    DX = D // NX
    ND = NY * NZ
    SECT = 2 * NX
    reach = KT // 2
    lanes_x = DX // 128

    dpi = lax.axis_index("dp")
    pipe = lax.axis_index("pipe")
    x, c = pipe // CORES, pipe % CORES
    y, z = dpi // NZ, dpi % NZ

    def dev(yy=None, zz=None, xx=None, cc=None):
        yy = y if yy is None else yy
        zz = z if zz is None else zz
        xx = x if xx is None else xx
        cc = c if cc is None else cc
        return {"dp": yy * NZ + zz, "pipe": xx * CORES + cc}

    sib = dev(cc=1 - c)
    xs_ = [(j, (x + j) % NX) for j in range(1, NX)]
    ys_ = [(j, (y + j) % NY) for j in range(1, NY)]
    zs_ = [(j, (z + j) % NZ) for j in range(1, NZ)]

    def half(h):
        return pl.ds(h * DX, DX)

    def cols(b):
        return pl.ds(pl.multiple_of(b * DX, 128), DX)

    barrier = pltpu.get_barrier_semaphore()
    peers = [sib]
    peers += [dev(xx=xx) for _, xx in xs_]
    peers += [dev(yy=yy) for _, yy in ys_]
    peers += [dev(zz=zz) for _, zz in zs_]
    for peer in peers:
        pl.semaphore_signal(barrier, inc=1, device_id=peer, device_id_type=pl.DeviceIdType.MESH)
    pl.semaphore_wait(barrier, len(peers))

    for j, xx in xs_:
        rcopy(mixing.at[0, :, cols(xx)], W.at[c, x, y, z, :, half(0)], xw_s.at[j], xw_r.at[x], dev(xx=xx)).start()
        rcopy(gating.at[0, :, cols(xx)], W.at[c, x, y, z, :, half(1)], xw_s.at[j], xw_r.at[x], dev(xx=xx)).start()
    own_copies = [
        pltpu.make_async_copy(mixing.at[0, :, cols(x)], W.at[c, x, y, z, :, half(0)], lw_s.at[0]),
        pltpu.make_async_copy(gating.at[0, :, cols(x)], W.at[c, x, y, z, :, half(1)], lw_s.at[1]),
    ]
    for copy in own_copies:
        copy.start()

    for j, yy in ys_:
        rcopy(slabs.at[pl.ds(yy * NZ, NZ)], T1.at[y], tl_s.at[0, j], tl_r.at[0, y], dev(yy=yy)).start()
    T1[y] = slabs[pl.ds(y * NZ, NZ)]

    for j, xx in xs_:
        rcopy(tg.at[:, cols(xx)], TAPS.at[c, x], tg_s.at[0, j], tg_r.at[0, x], dev(xx=xx)).start()
        rcopy(gain8, GAIN.at[c, x], tg_s.at[1, j], tg_r.at[1, x], dev(xx=xx)).start()
    TAPS[c, x] = tg[:, cols(x)]
    GAIN[c, x] = gain8[...]

    for j, yy in ys_:
        rcopy(slabs.at[pl.ds(yy * NZ, NZ)], T1.at[yy], tl_s.at[0, j], tl_r.at[0, yy], dev(yy=yy)).wait()
    for j, zz in zs_:
        rcopy(T1.at[:, zz], T2.at[z], tl_s.at[1, j], tl_r.at[1, z], dev(zz=zz)).start()
    T2[z] = T1[:, z]

    for copy in own_copies:
        copy.wait()
    for j, xx in xs_:
        rcopy(W.at[c, x, y, z], W.at[c, xx, y, z], xw_s.at[j], xw_r.at[xx], dev(xx=xx)).wait()

    def gather(cc):
        n1, n2 = (NY, NZ) if cc == 0 else (NZ, NY)
        me1, me2 = (y, z) if cc == 0 else (z, y)

        def block1(i, j, h):
            return W.at[cc, i, j, z, :, half(h)] if cc == 0 else W.at[cc, i, y, j, :, half(h)]

        def block2(i, j, h):
            return W.at[cc, i, :, j, :, half(h)] if cc == 0 else W.at[cc, i, j, :, :, half(h)]

        def neighbour(phase, me, sgn, n):
            pos = (me + sgn + n) % n
            along_y = (phase == 0) == (cc == 0)
            return dev(yy=pos) if along_y else dev(zz=pos)

        def ring(phase, n, me, block, forward):
            def start(t, i):
                for h, sgn in ((0, 1), (1, -1)):
                    b = (me - sgn * (t - 1) + 2 * n) % n
                    rcopy(
                        block(i, b, h), block(i, b, h), ag_s.at[phase, i, h], ag_r.at[phase, i, h, t - 1],
                        neighbour(phase, me, sgn, n),
                    ).start()
                    if forward:
                        rcopy(block(i, b, h), block(i, b, h), sw_s.at[i], sw_r.at[i], sib).start()

            def arrived(t, i):
                for h, sgn in ((0, 1), (1, -1)):
                    b = (me - sgn * t + 2 * n) % n
                    rcopy(
                        block(i, b, h), block(i, b, h), ag_s.at[phase, i, h], ag_r.at[phase, i, h, t - 1],
                        neighbour(phase, me, sgn, n),
                    ).wait_recv()

            def loop(f):
                lax.fori_loop(0, NX, lambda i, _: (f(i), 0)[1], 0)

            loop(lambda i: start(1, i))

            def step(t, _):
                def one(i):
                    arrived(t, i)
                    start(t + 1, i)

                loop(one)
                return 0

            lax.fori_loop(1, n - 1, step, 0)

            def last(i):
                arrived(n - 1, i)
                if forward:
                    for h, sgn in ((0, 1), (1, -1)):
                        b = (me - sgn * (n - 1) + 2 * n) % n
                        rcopy(block(i, b, h), block(i, b, h), sw_s.at[i], sw_r.at[i], sib).start()

            loop(last)

        ring(0, n1, me1, block1, False)
        ring(1, n2, me2, block2, True)

        def drain(i, _):
            for h in range(2):
                if cc == 0:
                    first, second = W.at[cc, i, 0 : n1 - 1, 0, :, half(h)], W.at[cc, i, :, 0 : n2 - 1, :, half(h)]
                else:
                    first, second = W.at[cc, i, 0, 0 : n1 - 1, :, half(h)], W.at[cc, i, 0 : n2 - 1, :, :, half(h)]
                rcopy(first, first, ag_s.at[0, i, h], ag_r.at[0, i, h, 0], sib).wait_send()
                rcopy(second, second, ag_s.at[1, i, h], ag_r.at[1, i, h, 0], sib).wait_send()
            return 0

        lax.fori_loop(0, NX, drain, 0)

    for cc in range(CORES):
        pl.when(c == cc)(functools.partial(gather, cc))

    for j, xx in xs_:
        rcopy(tg.at[:, cols(xx)], TAPS.at[c, xx], tg_s.at[0, j], tg_r.at[0, xx], dev(xx=xx)).wait()
        rcopy(gain8, GAIN.at[c, xx], tg_s.at[1, j], tg_r.at[1, xx], dev(xx=xx)).wait()
    taps_out = rcopy(TAPS.at[c], TAPS.at[c], st_s.at[0], st_r.at[0], sib)
    gain_out = rcopy(GAIN.at[c], GAIN.at[c], st_s.at[1], st_r.at[1], sib)
    taps_out.start()
    gain_out.start()

    for j, zz in zs_:
        rcopy(T1.at[:, zz], T2.at[zz], tl_s.at[1, j], tl_r.at[1, zz], dev(zz=zz)).wait()
    TF[...] = T2[...].astype(F32).reshape(TF.shape)
    for f in range(TSUB):
        for j in range(J):
            EA[f * ND : (f + 1) * ND, j * 128 : (j + 1) * 128] = TF[:, f * J + j, :]
    embedded = jnp.dot(EA[...].astype(BF16), sub[...], preferred_element_type=F32).astype(BF16)
    detail = TF[:, TSUB * J, :]
    rows = TSUB * ND
    detail_rows = jnp.concatenate([detail] * TSUB, axis=0)
    slot, label, length = (detail_rows[:, k : k + 1] for k in range(3))
    frame_in_tile = (lax.broadcasted_iota(jnp.int32, (rows, 1), 0) // ND).astype(F32)
    time_lane = lax.broadcasted_iota(jnp.int32, (rows, FRM), 1)
    first_slot = (c * (FRM // TSUB)).astype(F32)
    pick = (slot - first_slot == (time_lane // TSUB).astype(F32)) & (
        frame_in_tile == (time_lane % TSUB).astype(F32)
    )
    pick = pick.astype(F32).astype(BF16)
    placed = lax.dot_general(pick, embedded, (((0,), (0,)), ((), ())), preferred_element_type=F32).astype(BF16)
    for b in range(NX):
        X[0, b] = placed[:, b * DX : (b + 1) * DX]
    code_rows = jnp.broadcast_to(jnp.where(frame_in_tile < length, label, -1.0), (rows, 128)).astype(BF16)
    code = lax.dot_general(pick, code_rows, (((0,), (0,)), ((), ())), preferred_element_type=F32)
    CP[...] = jnp.full(CP.shape, -2.0, F32)
    CP[16 : 16 + FRM] = code
    for k in range(KT):
        start = 16 - reach + k
        MASK[k] = jnp.where((CP[start : start + FRM] == code) & (code >= 0.0), 1.0, 0.0)
    edge = jnp.zeros((16, DX), F32)
    SP[0:16] = edge
    SP[16 + FRM :] = edge

    def clear(s, _):
        GL[s, 0:16] = edge
        GL[s, 16 + FRM :] = edge
        return 0

    lax.fori_loop(0, SECT, clear, 0)

    rcopy(TAPS.at[1 - c], TAPS.at[1 - c], st_s.at[0], st_r.at[0], sib).wait_recv()
    rcopy(GAIN.at[1 - c], GAIN.at[1 - c], st_s.at[1], st_r.at[1], sib).wait_recv()

    def statistics(s):
        blocks = [X[s, b].astype(F32) for b in range(NX)]
        mean = sum(jnp.sum(v, axis=1, keepdims=True) for v in blocks) * (1.0 / D)
        shifted = [v - mean for v in blocks]
        spread = sum(jnp.sum(v * v, axis=1, keepdims=True) for v in shifted) * (1.0 / D)
        return mean, shifted, lax.rsqrt(spread + EPSILON)

    def weight(s):
        return W[s % 2, s // 2].reshape(D, 2 * DX)

    def forward(s, _):
        @pl.when(s % 2 != c)
        def _():
            there = W.at[1 - c, s // 2]
            rcopy(there, there, sw_s.at[s // 2], sw_r.at[s // 2], sib).wait_recv()

        @pl.when(s > 0)
        def _():
            for j, xx in xs_:
                rcopy(X.at[s, x], X.at[s, xx], xf_s.at[s, j], xf_r.at[s, xx], dev(xx=xx)).wait()

        _, shifted, inverse = statistics(s)
        for b in range(NX):
            gain = GAIN[s % 2, s // 2, 0:1, b * DX : (b + 1) * DX]
            NT[s, :, b * DX : (b + 1) * DX] = (shifted[b] * inverse * gain).astype(BF16)

        @pl.when(s % 2 != c)
        def _():
            rcopy(NT.at[s], NS.at[s // 2], sn_s.at[s // 2], sn_r.at[s // 2], sib).start()

        both = jnp.dot(NT[s], weight(s), preferred_element_type=F32)
        value, gate = both[:, :DX], both[:, DX:]
        sig = jax.nn.sigmoid(gate)
        V[s] = value
        SG[s] = sig
        GL[s, 16 : 16 + FRM] = value * sig
        for tile in range(lanes_x):
            lane = slice(tile * 128, (tile + 1) * 128)
            total = jnp.zeros((FRM, 128), F32)
            for k in range(KT):
                start = 16 - reach + k
                total = total + GL[s, start : start + FRM, lane] * MASK[k] * TAPS[s % 2, s // 2, k : k + 1, lane]
            CV[s, :, lane] = total
        conv = CV[s]
        result = X[s, x].astype(F32) + conv * jax.nn.sigmoid(conv)

        @pl.when(s < SECT - 1)
        def _():
            X[s + 1, x] = result.astype(BF16)
            for j, xx in xs_:
                rcopy(X.at[s + 1, x], X.at[s + 1, x], xf_s.at[s + 1, j], xf_r.at[s + 1, x], dev(xx=xx)).start()

        return 0

    lax.fori_loop(0, SECT, forward, 0)

    GC[...] = cot[pl.ds(pl.multiple_of(c * FRM, 16), FRM), cols(x)].astype(F32)

    def weight_gradient(s):
        i = s // 2
        rcopy(NT.at[s], NS.at[i], sn_s.at[i], sn_r.at[i], sib).wait_recv()
        rcopy(GO.at[s], GS.at[i], sg_s.at[i], sg_r.at[i], sib).wait_recv()
        grads = jnp.concatenate([GO[s], GS[i]], axis=0)
        width = D // NY
        for part in range(NY):
            lane = slice(part * width, (part + 1) * width)
            normed = jnp.concatenate([NT[s, :, lane], NS[i, :, lane]], axis=0)
            product = lax.dot_general(normed, grads, (((0,), (0,)), ((), ())), preferred_element_type=F32)
            G[i, part] = product.astype(BF16).reshape(NZ, R, 2 * DX)

    def backward(step, _):
        s = SECT - 1 - step
        par, i = s % 2, s // 2
        conv = CV[s]
        sig_conv = jax.nn.sigmoid(conv)
        seed = GC[...]
        SP[16 : 16 + FRM] = seed * (sig_conv * (1.0 + conv * (1.0 - sig_conv)))
        for tile in range(lanes_x):
            lane = slice(tile * 128, (tile + 1) * 128)
            total = jnp.zeros((FRM, 128), F32)
            for k in range(KT):
                start = 16 - reach + k
                total = total + SP[start : start + FRM, lane] * MASK[k] * TAPS[par, i, KT - 1 - k : KT - k, lane]
            grad_value = total * SG[s, :, lane]
            grad_gate = grad_value * V[s, :, lane] * (1.0 - SG[s, :, lane])
            GO[s, :, lane] = grad_value.astype(BF16)
            GO[s, :, DX + tile * 128 : DX + (tile + 1) * 128] = grad_gate.astype(BF16)

        @pl.when(par != c)
        def _():
            rcopy(GO.at[s], GS.at[i], sg_s.at[i], sg_r.at[i], sib).start()

        partial = lax.dot_general(GO[s], weight(s), (((1,), (1,)), ((), ())), preferred_element_type=F32)
        mean, shifted, inverse = statistics(s)
        sum_a = jnp.zeros((FRM, 1), F32)
        sum_b = jnp.zeros((FRM, 1), F32)
        for b in range(NX):
            block = partial[:, b * DX : (b + 1) * DX]
            PF[b] = block
            MS[s, b, :, :DX] = block.astype(BF16)
            scaled = block * GAIN[par, i, 0:1, b * DX : (b + 1) * DX]
            sum_a = sum_a + jnp.sum(scaled, axis=1, keepdims=True)
            sum_b = sum_b + jnp.sum(scaled * (shifted[b] * inverse), axis=1, keepdims=True)
        lane_id = lax.broadcasted_iota(jnp.int32, (FRM, 128), 1)
        high_a, high_b = sum_a.astype(BF16).astype(F32), sum_b.astype(BF16).astype(F32)
        packed = jnp.where(lane_id == 0, high_a, 0.0)
        packed = jnp.where(lane_id == 1, sum_a - high_a, packed)
        packed = jnp.where(lane_id == 2, high_b, packed)
        packed = jnp.where(lane_id == 3, sum_b - high_b, packed).astype(BF16)
        for b in range(NX):
            MS[s, b, :, DX:] = packed
        for j, xx in xs_:
            rcopy(MS.at[s, xx], MR.at[s, x], xb_s.at[s, j], xb_r.at[s, x], dev(xx=xx)).start()

        for tile in range(lanes_x):
            lane = slice(tile * 128, (tile + 1) * 128)
            spread = SP[16 : 16 + FRM, lane]
            for k in range(KT):
                start = 16 - reach + k
                TT[s, k : k + 1, lane] = jnp.sum(
                    spread * GL[s, start : start + FRM, lane] * MASK[k], axis=0, keepdims=True
                )

        @pl.when((par != c) & (step > 0))
        def _():
            weight_gradient(s + 1)

        for j, xx in xs_:
            rcopy(MS.at[s, xx], MR.at[s, xx], xb_s.at[s, j], xb_r.at[s, xx], dev(xx=xx)).wait()
        total = PF[x]
        for j, xx in xs_:
            total = total + MR[s, xx, :, :DX].astype(F32)
            packed = MR[s, xx, :, DX:].astype(F32)
            sum_a = sum_a + packed[:, 0:1] + packed[:, 1:2]
            sum_b = sum_b + packed[:, 2:3] + packed[:, 3:4]
        xhat = (X[s, x].astype(F32) - mean) * inverse
        TT[s, KT : KT + 1, :] = jnp.sum(total * xhat, axis=0, keepdims=True)
        gain = GAIN[par, i, 0:1, cols(x)]
        grad_in = inverse * (total * gain - sum_a * (1.0 / D) - xhat * (sum_b * (1.0 / D)))
        GC[...] = (GC[...] + grad_in).astype(BF16).astype(F32)
        return 0

    lax.fori_loop(0, SECT, backward, 0)

    pl.when(c == 0)(lambda: weight_gradient(0))

    for i in range(NX):
        rcopy(TT.at[2 * i + 1 - c], TS.at[i], tt_s.at[4, i], tt_r.at[4, i], sib).start()

    def scatter(cc):
        n1, n2 = (NY, NZ) if cc == 0 else (NZ, NY)
        me1, me2 = (y, z) if cc == 0 else (z, y)
        dirs = ((0, 1), (1, -1))

        def region(i, j, h):
            return G.at[i, :, j, :, half(h)] if cc == 0 else G.at[i, j, :, :, half(h)]

        def region_value(i, j, h):
            return G[i, :, j, :, half(h)] if cc == 0 else G[i, j, :, :, half(h)]

        def neighbour(phase, sgn):
            me, n = (me2, n2) if phase == 0 else (me1, n1)
            pos = (me + sgn + n) % n
            along_z = (phase == 0) == (cc == 0)
            return dev(zz=pos) if along_z else dev(yy=pos)

        def slot_a(i, h, t):
            return RA.at[i, h, pl.ds((t - 1) * n1, n1)]

        def send_a(i, h, sgn, src, t):
            return rcopy(src, slot_a(i, h, t), rs_s.at[0, i, h], rs_r.at[0, i, h, t - 1], neighbour(0, sgn))

        def loop(f):
            lax.fori_loop(0, NX, lambda i, _: (f(i), 0)[1], 0)

        def first_a(i):
            for h, sgn in dirs:
                send_a(i, h, sgn, region(i, (me2 - sgn + n2) % n2, h), 1).start()

        loop(first_a)

        def add_a(i, h, sgn, t):
            send_a(i, h, sgn, slot_a(i, h, t), t).wait_recv()
            target = (me2 - sgn * (t + 1) + 2 * n2) % n2
            held = pl.ds((t - 1) * n1, n1)
            RA[i, h, held] = (RA[i, h, held].astype(F32) + region_value(i, target, h).astype(F32)).astype(BF16)

        def step_a(t, _):
            def one(i):
                for h, sgn in dirs:
                    add_a(i, h, sgn, t)
                    send_a(i, h, sgn, slot_a(i, h, t), t + 1).start()

            loop(one)
            return 0

        lax.fori_loop(1, n2 - 1, step_a, 0)

        base = (n2 - 2) * n1

        def send_b(i, h, sgn, src, t):
            return rcopy(src, RB.at[i, h, t - 1], rs_s.at[1, i, h], rs_r.at[1, i, h, t - 1], neighbour(1, sgn))

        def last_a(i):
            for h, sgn in dirs:
                add_a(i, h, sgn, n2 - 1)
                send_b(i, h, sgn, RA.at[i, h, base + (me1 - sgn + n1) % n1], 1).start()

        loop(last_a)

        def add_b(i, h, sgn, t):
            send_b(i, h, sgn, RB.at[i, h, t - 1], t).wait_recv()
            target = (me1 - sgn * (t + 1) + 2 * n1) % n1
            return RB[i, h, t - 1].astype(F32) + RA[i, h, base + target].astype(F32)

        def step_b(t, _):
            def one(i):
                for h, sgn in dirs:
                    RB[i, h, t - 1] = add_b(i, h, sgn, t).astype(BF16)
                    send_b(i, h, sgn, RB.at[i, h, t - 1], t + 1).start()

            loop(one)
            return 0

        lax.fori_loop(1, n1 - 1, step_b, 0)

        def last_b(i):
            for h, sgn in dirs:
                FS[i, :, half(h)] = add_b(i, h, sgn, n1 - 1).astype(BF16)

        loop(last_b)

        def drain(i, _):
            for h in range(2):
                sent_a, sent_b = RA.at[i, h, 0 : (n2 - 1) * n1], RB.at[i, h, 0 : n1 - 1]
                rcopy(sent_a, sent_a, rs_s.at[0, i, h], rs_r.at[0, i, h, 0], sib).wait_send()
                rcopy(sent_b, sent_b, rs_s.at[1, i, h], rs_r.at[1, i, h, 0], sib).wait_send()
            return 0

        lax.fori_loop(0, NX, drain, 0)

    for cc in range(CORES):
        pl.when(c == cc)(functools.partial(scatter, cc))

    for j, xx in xs_:
        rcopy(FS.at[xx], FR.at[x], fin_s.at[j], fin_r.at[x], dev(xx=xx)).start()
    FR[x] = FS[x]

    for i in range(NX):
        rcopy(TT.at[2 * i + 1 - c], TS.at[i], tt_s.at[4, i], tt_r.at[4, i], sib).wait()
    TY[...] = jnp.zeros(TY.shape, F32)
    for i in range(NX):
        summed = TT[2 * i + c] + TS[i]
        for r in range(KT + 1):
            TY[r // NZ, r % NZ, i : i + 1, :] = summed[r : r + 1]
    for j, yy in ys_:
        rcopy(TY.at[yy], TYR.at[y], tt_s.at[0, j], tt_r.at[0, y], dev(yy=yy)).start()
    TYR[y] = TY[y]
    for j, yy in ys_:
        rcopy(TY.at[yy], TYR.at[yy], tt_s.at[0, j], tt_r.at[0, yy], dev(yy=yy)).wait()
    TY[y] = sum(TYR[k] for k in range(NY))
    for j, zz in zs_:
        rcopy(TY.at[y, zz], TZR.at[z], tt_s.at[1, j], tt_r.at[1, z], dev(zz=zz)).start()
    TZR[z] = TY[y, z]
    for j, zz in zs_:
        rcopy(TY.at[y, zz], TZR.at[zz], tt_s.at[1, j], tt_r.at[1, zz], dev(zz=zz)).wait()
    TX[...] = sum(TZR[k] for k in range(NZ))
    for j, xx in xs_:
        rcopy(TX, TXR.at[x], tt_s.at[2, j], tt_r.at[2, x], dev(xx=xx)).start()
    TXR[x] = TX[...]
    for j, xx in xs_:
        rcopy(TX, TXR.at[xx], tt_s.at[2, j], tt_r.at[2, xx], dev(xx=xx)).wait()
    TO1[z] = jnp.zeros(TO1.shape[1:], F32)
    mine = lax.broadcasted_iota(jnp.int32, (8, DX), 0) == x
    for b in range(NX):
        row = jnp.sum(jnp.where(mine, TXR[b], 0.0), axis=0, keepdims=True)
        for tile in range(lanes_x):
            k = b * lanes_x + tile
            TO1[z, k : k + 1, :] = row[:, tile * 128 : (tile + 1) * 128]
    for j, zz in zs_:
        rcopy(TO1.at[z], TO1.at[z], tt_s.at[3, j], tt_r.at[3, z], dev(zz=zz)).start()
    for j, zz in zs_:
        rcopy(TO1.at[z], TO1.at[zz], tt_s.at[3, j], tt_r.at[3, zz], dev(zz=zz)).wait()
    for j, yy in ys_:
        rcopy(TO1, TO2.at[y], tt_s.at[5, j], tt_r.at[5, y], dev(yy=yy)).start()
    TO2[y] = TO1[...]
    for j, yy in ys_:
        rcopy(TO1, TO2.at[yy], tt_s.at[5, j], tt_r.at[5, yy], dev(yy=yy)).wait()
    o_taps[...] = TO2[...].reshape(o_taps.shape)

    for j, xx in xs_:
        rcopy(FS.at[xx], FR.at[xx], fin_s.at[j], fin_r.at[xx], dev(xx=xx)).wait()
    for b in range(NX):
        o_mix[0, :, b * DX : (b + 1) * DX] = FR[b, :, :DX].astype(F32)
        o_gate[0, :, b * DX : (b + 1) * DX] = FR[b, :, DX:].astype(F32)

    taps_out.wait_send()
    gain_out.wait_send()

    def drain(i, _):
        there = W.at[c, i]
        rcopy(there, there, sw_s.at[i], sw_r.at[i], sib).wait_send()
        rcopy(NT.at[0], NS.at[i], sn_s.at[i], sn_r.at[i], sib).wait_send()
        rcopy(GO.at[0], GS.at[i], sg_s.at[i], sg_r.at[i], sib).wait_send()
        return 0

    lax.fori_loop(0, NX, drain, 0)


def body(
    mel_tiles,
    utt_ids,
    tile_lengths,
    dest_shard,
    dest_slot,
    subsample_weight,
    mixing_weight,
    gate_weight,
    conv_taps,
    norm_gain,
    out_cot,
):
    ND = lax.axis_size("dp")
    SECT = lax.axis_size("pipe")
    NX = SECT // CORES
    NY, NZ = PHYS[ND]
    tiles, TSUB, feats = mel_tiles.shape
    D = subsample_weight.shape[1]
    KT = conv_taps.shape[1]
    R = mixing_weight.shape[1]
    FRM = tiles * TSUB // 2
    J = -(-feats // 128)
    DX = D // NX
    SR = -(-(TSUB * J + 1) // 16) * 16
    dims = dict(X=NX, Y=NY, Z=NZ, D=D, R=R, F=FRM, TSUB=TSUB, J=J, TAPS=KT)

    details = jnp.stack([dest_slot, utt_ids, tile_lengths], axis=1).astype(BF16)
    flat = jnp.concatenate(
        [
            jnp.pad(mel_tiles, ((0, 0), (0, 0), (0, J * 128 - feats))).reshape(tiles, TSUB * J * 128),
            jnp.pad(details, ((0, 0), (0, 125 + (SR - TSUB * J - 1) * 128))),
        ],
        axis=1,
    )
    order = (dest_shard[None, :] == jnp.arange(ND, dtype=jnp.int32)[:, None]).astype(BF16)
    slabs = jnp.dot(order, flat, preferred_element_type=F32).astype(BF16).reshape(ND, SR, 128)
    tg = jnp.concatenate([conv_taps[0], norm_gain], axis=0)
    gain8 = jnp.broadcast_to(norm_gain, (8, D))
    sub = jnp.pad(subsample_weight, ((0, J * 128 - feats), (0, 0)))
    OR = -(-(D // 128) // 8) * 8
    NR = max(NY, NZ) - 1

    def vm(shape, kind=F32):
        return pltpu.VMEM(shape, kind)

    def sems(*shape):
        return pltpu.SemaphoreType.DMA(shape)

    scratch = [
        vm((2, NX, NY, NZ, R, 2 * DX), BF16),
        vm((2, NX, KT + 1, DX)),
        vm((2, NX, 8, D)),
        vm((NY, NZ, SR, 128), BF16),
        vm((NZ, NY, SR, 128), BF16),
        vm((ND, SR, 128)),
        vm((TSUB * ND, J * 128)),
        vm((FRM + 32, 128)),
        vm((KT, FRM, 128)),
        vm((SECT, NX, FRM, DX), BF16),
        vm((SECT, FRM, D), BF16),
        vm((NX, FRM, D), BF16),
        vm((SECT, FRM + 32, DX)),
        vm((FRM + 32, DX)),
        vm((SECT, FRM, DX)),
        vm((SECT, FRM, DX)),
        vm((SECT, FRM, DX)),
        vm((FRM, DX)),
        vm((NX, FRM, DX)),
        vm((SECT, FRM, 2 * DX), BF16),
        vm((NX, FRM, 2 * DX), BF16),
        vm((SECT, NX, FRM, DX + 128), BF16),
        vm((SECT, NX, FRM, DX + 128), BF16),
        vm((NX, NY, NZ, R, 2 * DX), BF16),
        vm((NX, 2, max((NZ - 1) * NY, (NY - 1) * NZ), R, DX), BF16),
        vm((NX, 2, NR, R, DX), BF16),
        vm((NX, R, 2 * DX), BF16),
        vm((NX, R, 2 * DX), BF16),
        vm((SECT, KT + 1, DX)),
        vm((NX, KT + 1, DX)),
        vm((NY, NZ, 8, DX)),
        vm((NY, NZ, 8, DX)),
        vm((NZ, 8, DX)),
        vm((8, DX)),
        vm((NX, 8, DX)),
        vm((NZ, OR, 128)),
        vm((NY, NZ, OR, 128)),
        sems(2),
        sems(NX),
        sems(NX),
        sems(2, NX),
        sems(2, NX),
        sems(2, max(NY, NZ)),
        sems(2, max(NY, NZ)),
        sems(2, NX, 2),
        sems(2, NX, 2, NR),
        sems(2, NX, 2),
        sems(2, NX, 2, NR),
        sems(NX),
        sems(NX),
        sems(2),
        sems(2),
        sems(SECT, NX),
        sems(SECT, NX),
        sems(SECT, NX),
        sems(SECT, NX),
        sems(NX),
        sems(NX),
        sems(NX),
        sems(NX),
        sems(NX),
        sems(NX),
        sems(6, max(NX, NY, NZ)),
        sems(6, max(NX, NY, NZ)),
    ]
    in_vmem = pl.BlockSpec(memory_space=pltpu.VMEM)
    in_any = pl.BlockSpec(memory_space=pl.ANY)
    mix, gate, taps = pl.pallas_call(
        functools.partial(kernel, dims),
        out_shape=(
            jax.ShapeDtypeStruct((1, R, D), F32),
            jax.ShapeDtypeStruct((1, R, D), F32),
            jax.ShapeDtypeStruct((ND, OR, 128), F32),
        ),
        in_specs=[in_vmem, in_any, in_any, in_vmem, in_vmem, in_vmem, in_vmem],
        out_specs=(in_vmem, in_vmem, in_vmem),
        scratch_shapes=scratch,
        compiler_params=pltpu.CompilerParams(
            collective_id=0, has_side_effects=True, vmem_limit_bytes=VMEM_LIMIT
        ),
    )(slabs, mixing_weight, gate_weight, tg, gain8, sub, out_cot)
    rows = taps[:, : D // 128].reshape(ND, D)
    return mix, gate, rows[None, :KT], rows[KT:]


def solution(mesh):
    in_specs = (
        P("dp", None, None),
        P("dp"),
        P("dp"),
        P("dp"),
        P("dp"),
        P(),
        P("pipe", "dp", None),
        P("pipe", "dp", None),
        P("pipe", None, None),
        P("pipe", None),
        P("dp", None),
    )
    out_specs = (
        P("pipe", "dp", None),
        P("pipe", "dp", None),
        P("pipe", None, None),
        P("pipe", None),
    )
    return jax.shard_map(body, mesh=mesh, in_specs=in_specs, out_specs=out_specs, check_vma=False)
```

time: 1050 us -> 291 us (0.28); the launches traced: 1030 us -> 290 us
  waiting for transfers between devices: 611 us -> 0 us
  Pallas kernels: 0 us -> 277 us
  local copies, waits for them, and re-layouts: 136 us -> 8.1 us
  starting transfers between devices: 99.7 us -> 0 us
  other arithmetic: 76.9 us -> 2.85 us
  blocking collectives: 64.5 us -> 0 us
  matrix products: 23.9 us -> 0.81 us
  between operations: 16 us -> 0.72 us
    pallas_call x0 -> x1, Pallas kernels: none -> 277 us  [body(): pl.pallas_call(functools.partial(kernel, dims), out_shape=(jax.ShapeDtype...]
    reduce_scatter x1 -> x0, waiting for transfers between devices: 232 us -> none  [body(): lax.psum_scatter(lax.dot_general(all_normed, all_grads, (((0,), (0,)), ((...]
    ppermute x16 -> x0, waiting for transfers between devices: 174 us -> none  [passed_along(): lax.ppermute(value, axis, [(source, source + steps) for source in range(i...]
    all_gather x2 -> x0, waiting for transfers between devices: 130 us -> none  [the longest x1 83.4 us: body(): lax.all_gather(gate_weight, 'dp', axis=1, tiled=True)]
    ppermute x16 -> x0, starting transfers between devices: 82.6 us -> none  [passed_along(): lax.ppermute(value, axis, [(source, source + steps) for source in range(i...]
    dynamic_update_slice x53 -> x0, local copies, waits for them, and re-layouts: 71.9 us -> none  [the longest x9 16.2 us: body(): lax.dynamic_update_index_in_dim(saved_spread, spread, target, 0)]
    psum x1 -> x0, waiting for transfers between devices: 64.6 us -> none  [body(): lax.psum(tap_total.astype(jnp.bfloat16), 'dp').astype(jnp.float32)]
    psum x1 -> x0, blocking collectives: 64.5 us -> none  [body(): lax.psum(gain_total.astype(jnp.bfloat16), 'dp').astype(jnp.float32)]
  transfers between devices with their start and end apart: 22 -> 0, of which waited for: 15 -> 0; matrix products, arithmetic and copies ran while one was open for 9% -> 0% of each run, Pallas kernels for 0% -> 0%
where the time goes in v1:
time: 291 us; the launch traced here: 290 us
  Pallas kernels  277 us (95%)
  local copies, waits for them, and re-layouts  8.1 us (3%)
    pallas_call x1, Pallas kernels, body(): pl.pallas_call(functools.partial(kernel, dims), out_shape=(jax.ShapeDtype...  277 us

profile of v1, /device:TPU:8, one launch (start us, length us, event | category | flops | bytes accessed | tf_op | source)
XLA Modules:
  0.0 289.8 jit_solution(9318433040067873780)
XLA Ops:
  0.6 0.0 copy-start.4
  0.6 0.0 copy-start.3
  0.7 0.0 copy-start
  0.7 0.8 convert_bitcast_fusion.2
  1.4 0.7 convert_bitcast_fusion
  2.1 0.1 copy.20
  2.2 0.7 reduce
  2.9 0.6 broadcast_in_dim.13.gain8
  3.6 0.9 pad.12
  4.5 0.8 fusion
  5.3 0.7 copy.22
  6.0 0.0 copy-done.3
  6.0 0.0 copy-done.4
  6.0 0.7 pad_maximum_fusion.tg
  6.7 0.0 copy-done
  6.7 1.1 pad.14.sub
  7.8 277.3 %shard_map.138 = (f32[1,48,1536]{2,1,0:T(8,128)}, f32[1,48,1536]{2,1,0:T(8,128)}, f32[32,16,128]{2,1,0:T(8,128)}) custom-call(bf16[32,16,128]{2,1,0:T(8,128)(2,1)} %bitcast.20, bf16[1,48,1536]{2,1,0:T(8,128)(2,1)} %mixing.1, bf16[1,48,1536]{2,1,0:T(8,128)(2,1)} %gating.1, f32[32,1536]{1,0:T(8,128)} %pad_maximum_fusion.tg, f32[8,1536]{1,0:T(8,128)} %broadcast_in_dim.13.gain8, ...), custom_call_target="tpu_custom_call" | custom-call | tf_op jit(solution)/shard_map/pallas_call | solution.py:729
  285.2 0.0 copy-start.2
  285.2 0.0 copy-start.1
  285.2 0.8 slice_bitcast_fusion
  286.0 1.0 slice.13
  286.9 0.9 broadcast_in_dim.15
  287.8 0.6 copy.27
  288.4 0.0 copy-done.2
  288.4 0.7 copy.30
  289.1 0.0 copy-done.1
  289.1 0.7 copy.31
  (3 shorter events, 0.0 us)
Async XLA Ops:
  0.6 5.4 %copy-start.4 = (f32[1,1536]{1,0:T(1,128)S(1)}, f32[1,1536]{1,0:T(1,128)}, u32[]{:S(2)}) copy-start(f32[1,1536]{1,0:T(1,128)} %param.20) | copy-start | bytes 18436
  0.6 5.4 %copy-start.3 = (f32[1,31,1536]{2,0,1:T(1,128)S(1)}, f32[1,31,1536]{2,0,1:T(1,128)}, u32[]{:S(2)}) copy-start(f32[1,31,1536]{2,0,1:T(1,128)} %param.19) | copy-start | bytes 571396
  0.7 6.1 %copy-start = (bf16[320,1536]{1,0:T(8,128)(2,1)S(1)}, bf16[320,1536]{1,0:T(8,128)(2,1)}, u32[]{:S(2)}) copy-start(bf16[320,1536]{1,0:T(8,128)(2,1)} %param.16) | copy-start | bytes 2949124
  285.2 3.2 %copy-start.2 = (f32[1,48,1536]{2,1,0:T(8,128)S(1)}, f32[1,48,1536]{2,1,0:T(8,128)}, u32[]{:S(2)}) copy-start(f32[1,48,1536]{2,1,0:T(8,128)} %get-tuple-element.24) | copy-start | bytes 884740
  285.2 3.9 %copy-start.1 = (f32[1,48,1536]{2,1,0:T(8,128)S(1)}, f32[1,48,1536]{2,1,0:T(8,128)}, u32[]{:S(2)}) copy-start(f32[1,48,1536]{2,1,0:T(8,128)} %get-tuple-element.25) | copy-start | bytes 884740

commit v2 on v1

--- a/solution.py
+++ b/solution.py
@@ -56,11 +56,14 @@
     SG,
     CV,
     GC,
+    CT,
     PF,
+    XH,
     GO,
     GS,
     MS,
     MR,
+    MT,
     G,
     RA,
     RB,
@@ -82,10 +85,14 @@
     tg_r,
     tl_s,
     tl_r,
-    ag_s,
-    ag_r,
-    rs_s,
-    rs_r,
+    p1_s,
+    p1_r,
+    p2_s,
+    p2_r,
+    ra_s,
+    ra_r,
+    rb_s,
+    rb_r,
     sw_s,
     sw_r,
     st_s,
@@ -94,6 +101,8 @@
     xf_r,
     xb_s,
     xb_r,
+    xt_s,
+    xt_r,
     sn_s,
     sn_r,
     sg_s,
@@ -125,6 +134,7 @@
 
     sib = dev(cc=1 - c)
     xs_ = [(j, (x + j) % NX) for j in range(1, NX)]
+    far_first = sorted(xs_, key=lambda item: -min(item[0], NX - item[0]))
     ys_ = [(j, (y + j) % NY) for j in range(1, NY)]
     zs_ = [(j, (z + j) % NZ) for j in range(1, NZ)]
 
@@ -147,6 +157,8 @@
         rcopy(mixing.at[0, :, cols(xx)], W.at[c, x, y, z, :, half(0)], xw_s.at[j], xw_r.at[x], dev(xx=xx)).start()
         rcopy(gating.at[0, :, cols(xx)], W.at[c, x, y, z, :, half(1)], xw_s.at[j], xw_r.at[x], dev(xx=xx)).start()
     own_copies = [
+        pltpu.make_async_copy(sub, G.at[0, 0 : NX // 2], lw_s.at[2]),
+        pltpu.make_async_copy(cot.at[pl.ds(pl.multiple_of(c * FRM, 16), FRM), cols(x)], CT, lw_s.at[3]),
         pltpu.make_async_copy(mixing.at[0, :, cols(x)], W.at[c, x, y, z, :, half(0)], lw_s.at[0]),
         pltpu.make_async_copy(gating.at[0, :, cols(x)], W.at[c, x, y, z, :, half(1)], lw_s.at[1]),
     ]
@@ -174,81 +186,112 @@
     for j, xx in xs_:
         rcopy(W.at[c, x, y, z], W.at[c, xx, y, z], xw_s.at[j], xw_r.at[xx], dev(xx=xx)).wait()
 
-    def gather(cc):
-        n1, n2 = (NY, NZ) if cc == 0 else (NZ, NY)
-        me1, me2 = (y, z) if cc == 0 else (z, y)
-
-        def block1(i, j, h):
-            return W.at[cc, i, j, z, :, half(h)] if cc == 0 else W.at[cc, i, y, j, :, half(h)]
-
-        def block2(i, j, h):
-            return W.at[cc, i, :, j, :, half(h)] if cc == 0 else W.at[cc, i, j, :, :, half(h)]
-
-        def neighbour(phase, me, sgn, n):
+    dirs = ((0, 1), (1, -1))
+
+    class Rings:
+        def __init__(self, cc):
+            self.cc = cc
+            self.n1, self.n2 = (NY, NZ) if cc == 0 else (NZ, NY)
+            self.me1, self.me2 = (y, z) if cc == 0 else (z, y)
+            self.h1, self.h2 = self.n1 // 2, self.n2 // 2
+            self.m = self.n1 // 2
+
+        def to(self, ring, sgn):
+            me, n = (self.me1, self.n1) if ring == 1 else (self.me2, self.n2)
             pos = (me + sgn + n) % n
-            along_y = (phase == 0) == (cc == 0)
-            return dev(yy=pos) if along_y else dev(zz=pos)
-
-        def ring(phase, n, me, block, forward):
-            def start(t, i):
-                for h, sgn in ((0, 1), (1, -1)):
-                    b = (me - sgn * (t - 1) + 2 * n) % n
-                    rcopy(
-                        block(i, b, h), block(i, b, h), ag_s.at[phase, i, h], ag_r.at[phase, i, h, t - 1],
-                        neighbour(phase, me, sgn, n),
-                    ).start()
-                    if forward:
-                        rcopy(block(i, b, h), block(i, b, h), sw_s.at[i], sw_r.at[i], sib).start()
-
-            def arrived(t, i):
-                for h, sgn in ((0, 1), (1, -1)):
-                    b = (me - sgn * t + 2 * n) % n
-                    rcopy(
-                        block(i, b, h), block(i, b, h), ag_s.at[phase, i, h], ag_r.at[phase, i, h, t - 1],
-                        neighbour(phase, me, sgn, n),
-                    ).wait_recv()
-
-            def loop(f):
-                lax.fori_loop(0, NX, lambda i, _: (f(i), 0)[1], 0)
-
-            loop(lambda i: start(1, i))
-
-            def step(t, _):
-                def one(i):
-                    arrived(t, i)
-                    start(t + 1, i)
-
-                loop(one)
+            return dev(yy=pos) if (ring == 1) == (self.cc == 0) else dev(zz=pos)
+
+        def near(self, u, d):
+            return u == d
+
+    def at(e):
+        return 1 + e // 2, e % 2
+
+    class Gather(Rings):
+        def block1(self, i, b, u):
+            return W.at[0, i, b, z, :, half(u)] if self.cc == 0 else W.at[1, i, y, b, :, half(u)]
+
+        def block2(self, i, b, u):
+            part = pl.ds(u * self.m, self.m)
+            return W.at[0, i, part, b] if self.cc == 0 else W.at[1, i, b, part]
+
+        def step(self, ring, t, u, i):
+            n, me, last, block, send, recv = (
+                (self.n1, self.me1, self.h1, self.block1, p1_s, p1_r)
+                if ring == 1
+                else (self.n2, self.me2, self.h2, self.block2, p2_s, p2_r)
+            )
+            for d, sgn in dirs:
+                held = block(i, (me - sgn * t + 2 * n) % n, u)
+
+                def copy(k):
+                    return rcopy(held, held, send.at[i, d, u], recv.at[i, d, u, k], self.to(ring, sgn))
+
+                def arrive():
+                    copy(t - 1).wait_recv()
+                    if ring == 2:
+                        rcopy(held, held, sw_s.at[i], sw_r.at[i], sib).start()
+
+                if isinstance(t, int) and t == 0:
+                    if ring == 2 and d == 0:
+                        rcopy(held, held, sw_s.at[i], sw_r.at[i], sib).start()
+                    if last > 1 or self.near(u, d):
+                        copy(0).start()
+                    continue
+                if self.near(u, d):
+                    pl.when(t <= last)(arrive)
+                    pl.when(t < last)(lambda: copy(t).start())
+                else:
+                    pl.when(t < last)(arrive)
+                    pl.when(t < last - 1)(lambda: copy(t).start())
+
+        def begin(self, ring, i):
+            for u in range(2):
+                self.step(ring, 0, u, i)
+
+        def drain(self):
+            def one(i, _):
+                for u in range(2):
+                    for d in range(2):
+                        far = 0 if self.near(u, d) else 1
+                        k1, k2 = self.h1 - far, self.h2 - far
+                        part = pl.ds(0, self.m)
+                        if k1 > 0:
+                            sent = W.at[0, i, 0:k1, 0, :, half(u)] if self.cc == 0 else W.at[1, i, 0, 0:k1, :, half(u)]
+                            rcopy(sent, sent, p1_s.at[i, d, u], p1_r.at[i, d, u, 0], sib).wait_send()
+                        if k2 > 0:
+                            sent = W.at[0, i, part, 0:k2] if self.cc == 0 else W.at[1, i, 0:k2, part]
+                            rcopy(sent, sent, p2_s.at[i, d, u], p2_r.at[i, d, u, 0], sib).wait_send()
                 return 0
 
-            lax.fori_loop(1, n - 1, step, 0)
-
-            def last(i):
-                arrived(n - 1, i)
-                if forward:
-                    for h, sgn in ((0, 1), (1, -1)):
-                        b = (me - sgn * (n - 1) + 2 * n) % n
-                        rcopy(block(i, b, h), block(i, b, h), sw_s.at[i], sw_r.at[i], sib).start()
-
-            loop(last)
-
-        ring(0, n1, me1, block1, False)
-        ring(1, n2, me2, block2, True)
-
-        def drain(i, _):
-            for h in range(2):
-                if cc == 0:
-                    first, second = W.at[cc, i, 0 : n1 - 1, 0, :, half(h)], W.at[cc, i, :, 0 : n2 - 1, :, half(h)]
-                else:
-                    first, second = W.at[cc, i, 0, 0 : n1 - 1, :, half(h)], W.at[cc, i, 0 : n2 - 1, :, :, half(h)]
-                rcopy(first, first, ag_s.at[0, i, h], ag_r.at[0, i, h, 0], sib).wait_send()
-                rcopy(second, second, ag_s.at[1, i, h], ag_r.at[1, i, h, 0], sib).wait_send()
-            return 0
-
-        lax.fori_loop(0, NX, drain, 0)
-
-    for cc in range(CORES):
-        pl.when(c == cc)(functools.partial(gather, cc))
+            lax.fori_loop(0, NX, one, 0)
+
+    gathers = [Gather(cc) for cc in range(CORES)]
+    most = max(NY, NZ)
+
+    def each(rings, f):
+        for cc in range(CORES):
+            pl.when(c == cc)(functools.partial(f, rings[cc]))
+
+    def begin(g):
+        g.begin(1, 0)
+        for e in range(2 * g.h1):
+            g.step(1, *at(e), 0)
+        g.begin(2, 0)
+        for i in range(1, NX):
+            g.begin(1, i)
+
+    def go_on(low, high, g):
+        for e in range(low, high):
+            if e < 2 * g.h2:
+                g.step(2, *at(e), 0)
+            if e < 2 * g.h1:
+                for i in range(1, NX):
+                    g.step(1, *at(e), i)
+            if e == 2 * g.h1 - 1 and NX > 1:
+                g.begin(2, 1)
+
+    each(gathers, begin)
 
     for j, xx in xs_:
         rcopy(tg.at[:, cols(xx)], TAPS.at[c, xx], tg_s.at[0, j], tg_r.at[0, xx], dev(xx=xx)).wait()
@@ -264,7 +307,14 @@
     for f in range(TSUB):
         for j in range(J):
             EA[f * ND : (f + 1) * ND, j * 128 : (j + 1) * 128] = TF[:, f * J + j, :]
-    embedded = jnp.dot(EA[...].astype(BF16), sub[...], preferred_element_type=F32).astype(BF16)
+
+    each(gathers, functools.partial(go_on, 0, 1))
+    stacked = EA[...].astype(BF16)
+    embedded = [
+        jnp.dot(stacked, G[0, k].reshape(J * 128, 2 * DX), preferred_element_type=F32).astype(BF16)
+        for k in range(NX // 2)
+    ]
+    embedded = jnp.concatenate(embedded, axis=1)
     detail = TF[:, TSUB * J, :]
     rows = TSUB * ND
     detail_rows = jnp.concatenate([detail] * TSUB, axis=0)
@@ -279,6 +329,8 @@
     placed = lax.dot_general(pick, embedded, (((0,), (0,)), ((), ())), preferred_element_type=F32).astype(BF16)
     for b in range(NX):
         X[0, b] = placed[:, b * DX : (b + 1) * DX]
+    each(gathers, functools.partial(go_on, 1, 3))
+
     code_rows = jnp.broadcast_to(jnp.where(frame_in_tile < length, label, -1.0), (rows, 128)).astype(BF16)
     code = lax.dot_general(pick, code_rows, (((0,), (0,)), ((), ())), preferred_element_type=F32)
     CP[...] = jnp.full(CP.shape, -2.0, F32)
@@ -296,9 +348,25 @@
         return 0
 
     lax.fori_loop(0, SECT, clear, 0)
+    each(gathers, functools.partial(go_on, 3, most))
 
     rcopy(TAPS.at[1 - c], TAPS.at[1 - c], st_s.at[0], st_r.at[0], sib).wait_recv()
     rcopy(GAIN.at[1 - c], GAIN.at[1 - c], st_s.at[1], st_r.at[1], sib).wait_recv()
+
+    def pump(s, q):
+        pair = s // 2 + 1
+
+        def one(g):
+            if g.cc == 0:
+                t, u, e = 1 + (s % 2) * 2 + q // 2, q % 2, (s % 2) * 4 + q
+            elif q % 2 == 0:
+                t, u, e = 1 + s % 2, q // 2, (s % 2) * 2 + q // 2
+            else:
+                return
+            pl.when((pair < NX) & (t <= g.h2))(lambda: g.step(2, t, u, pair))
+            pl.when((pair + 1 < NX) & (e == max(2 * g.h2 - 3, 0)))(lambda: g.begin(2, pair + 1))
+
+        each(gathers, one)
 
     def statistics(s):
         blocks = [X[s, b].astype(F32) for b in range(NX)]
@@ -330,33 +398,38 @@
         def _():
             rcopy(NT.at[s], NS.at[s // 2], sn_s.at[s // 2], sn_r.at[s // 2], sib).start()
 
+        pump(s, 0)
         both = jnp.dot(NT[s], weight(s), preferred_element_type=F32)
         value, gate = both[:, :DX], both[:, DX:]
         sig = jax.nn.sigmoid(gate)
         V[s] = value
         SG[s] = sig
         GL[s, 16 : 16 + FRM] = value * sig
+        pump(s, 1)
         for tile in range(lanes_x):
+            if tile == lanes_x // 2:
+                pump(s, 2)
             lane = slice(tile * 128, (tile + 1) * 128)
-            total = jnp.zeros((FRM, 128), F32)
+            conv = jnp.zeros((FRM, 128), F32)
             for k in range(KT):
                 start = 16 - reach + k
-                total = total + GL[s, start : start + FRM, lane] * MASK[k] * TAPS[s % 2, s // 2, k : k + 1, lane]
-            CV[s, :, lane] = total
-        conv = CV[s]
-        result = X[s, x].astype(F32) + conv * jax.nn.sigmoid(conv)
-
-        @pl.when(s < SECT - 1)
-        def _():
-            X[s + 1, x] = result.astype(BF16)
-            for j, xx in xs_:
-                rcopy(X.at[s + 1, x], X.at[s + 1, x], xf_s.at[s + 1, j], xf_r.at[s + 1, x], dev(xx=xx)).start()
-
+                conv = conv + GL[s, start : start + FRM, lane] * MASK[k] * TAPS[s % 2, s // 2, k : k + 1, lane]
+            CV[s, :, lane] = conv
+
+            @pl.when(s < SECT - 1)
+            def _():
+                result = X[s, x, :, lane].astype(F32) + conv * jax.nn.sigmoid(conv)
+                X[s + 1, x, :, lane] = result.astype(BF16)
+                piece = X.at[s + 1, x, :, lane]
+                for j, xx in far_first:
+                    rcopy(piece, piece, xf_s.at[s + 1, j], xf_r.at[s + 1, x], dev(xx=xx)).start()
+
+        pump(s, 3)
         return 0
 
     lax.fori_loop(0, SECT, forward, 0)
 
-    GC[...] = cot[pl.ds(pl.multiple_of(c * FRM, 16), FRM), cols(x)].astype(F32)
+    GC[...] = CT[...].astype(F32)
 
     def weight_gradient(s):
         i = s // 2
@@ -369,6 +442,103 @@
             normed = jnp.concatenate([NT[s, :, lane], NS[i, :, lane]], axis=0)
             product = lax.dot_general(normed, grads, (((0,), (0,)), ((), ())), preferred_element_type=F32)
             G[i, part] = product.astype(BF16).reshape(NZ, R, 2 * DX)
+
+    class Scatter(Rings):
+        def own2(self, i, b, u):
+            part = pl.ds(u * self.m, self.m)
+            return G.at[i, part, b] if self.cc == 0 else G.at[i, b, part]
+
+        def own1(self, i, b, u):
+            return RA.at[i, 0, (self.h2 - 1) * self.n1 + b, :, half(u)]
+
+        def held2(self, i, d, t, u):
+            return RA.at[i, d, pl.ds((t - 1) * self.n1 + u * self.m, self.m)]
+
+        def held1(self, i, d, t, u):
+            return RB.at[i, d, t - 1, :, half(u)]
+
+        def step(self, ring, t, u, i):
+            n, me, last, own, held, send, recv = (
+                (self.n1, self.me1, self.h1, self.own1, self.held1, rb_s, rb_r)
+                if ring == 1
+                else (self.n2, self.me2, self.h2, self.own2, self.held2, ra_s, ra_r)
+            )
+            for d, sgn in dirs:
+                mine = own(i, (me + sgn * (last - t) + 2 * n) % n, u)
+                near = self.near(u, d)
+
+                def onward(src):
+                    return rcopy(src, held(i, d, t + 1, u), send.at[i, d, u], recv.at[i, d, u, t], self.to(ring, sgn))
+
+                if isinstance(t, int) and t == 0:
+                    if near:
+                        onward(mine).start()
+                    continue
+
+                def arrive():
+                    there = held(i, d, t, u)
+                    rcopy(there, there, send.at[i, d, u], recv.at[i, d, u, t - 1], self.to(ring, sgn)).wait_recv()
+
+                    @pl.when(t < last)
+                    def _():
+                        there[...] = (there[...].astype(F32) + mine[...].astype(F32)).astype(BF16)
+                        onward(there).start()
+
+                if near:
+                    arrive()
+                else:
+                    pl.when((t == 1) & (t < last))(lambda: onward(mine).start())
+                    pl.when(t > 1)(arrive)
+
+            @pl.when(t == last)
+            def _():
+                total = own(i, me, u)[...].astype(F32)
+                for d in range(2):
+                    if last > 1 or self.near(u, d):
+                        total = total + held(i, d, last, u)[...].astype(F32)
+                if ring == 1:
+                    FS[i, :, half(u)] = total.astype(BF16)
+                else:
+                    held(i, 0, last, u)[...] = total.astype(BF16)
+
+        def begin(self, ring, i):
+            for u in range(2):
+                self.step(ring, 0, u, i)
+
+        def drain(self):
+            def one(i, _):
+                for u in range(2):
+                    for d in range(2):
+                        far = 0 if self.near(u, d) else 1
+                        k1, k2 = self.h1 - far, self.h2 - far
+                        if k1 > 0:
+                            sent = RB.at[i, d, 0:k1, :, half(u)]
+                            rcopy(sent, sent, rb_s.at[i, d, u], rb_r.at[i, d, u, 0], sib).wait_send()
+                        if k2 > 0:
+                            sent = RA.at[i, d, 0 : k2 * self.m]
+                            rcopy(sent, sent, ra_s.at[i, d, u], ra_r.at[i, d, u, 0], sib).wait_send()
+                return 0
+
+            lax.fori_loop(0, NX, one, 0)
+
+    scatters = [Scatter(cc) for cc in range(CORES)]
+
+    def pump_back(s, q):
+        k = s // 2
+
+        def one(g):
+            if g.cc == 0:
+                odd = {0: (5, 2), 1: (6, 2), 2: (7, 2), 3: (0, 1)}[q]
+                even = (1 + q, 1)
+            else:
+                odd = {0: (0, 1), 2: (1, 1)}.get(q)
+                even = {0: (2, 1), 2: (3, 1)}.get(q)
+            for parity, what in ((1, odd), (0, even)):
+                if what is not None and what[0] < 2 * g.h2:
+                    e, ahead = what
+                    pl.when((s % 2 == parity) & (k + ahead < NX))(lambda: g.step(2, *at(e), k + ahead))
+
+        each(scatters, one)
 
     def backward(step, _):
         s = SECT - 1 - step
@@ -392,28 +562,34 @@
         def _():
             rcopy(GO.at[s], GS.at[i], sg_s.at[i], sg_r.at[i], sib).start()
 
-        partial = lax.dot_general(GO[s], weight(s), (((1,), (1,)), ((), ())), preferred_element_type=F32)
+        pump_back(s, 0)
         mean, shifted, inverse = statistics(s)
+        for b in range(NX):
+            XH[b] = shifted[b] * inverse
         sum_a = jnp.zeros((FRM, 1), F32)
         sum_b = jnp.zeros((FRM, 1), F32)
-        for b in range(NX):
-            block = partial[:, b * DX : (b + 1) * DX]
-            PF[b] = block
-            MS[s, b, :, :DX] = block.astype(BF16)
-            scaled = block * GAIN[par, i, 0:1, b * DX : (b + 1) * DX]
+        per = NY // NX
+        for j, xx in far_first + [(0, x)]:
+            rows_w = W[par, i, pl.ds(xx * per, per)].reshape(DX, 2 * DX)
+            block = lax.dot_general(GO[s], rows_w, (((1,), (1,)), ((), ())), preferred_element_type=F32)
+            if j == 0:
+                PF[...] = block
+            else:
+                MS[xx] = block.astype(BF16)
+                rcopy(MS.at[xx], MR.at[par, x], xb_s.at[s, j], xb_r.at[s, x], dev(xx=xx)).start()
+            scaled = block * GAIN[par, i, 0:1, cols(xx)]
             sum_a = sum_a + jnp.sum(scaled, axis=1, keepdims=True)
-            sum_b = sum_b + jnp.sum(scaled * (shifted[b] * inverse), axis=1, keepdims=True)
+            sum_b = sum_b + jnp.sum(scaled * XH[xx], axis=1, keepdims=True)
         lane_id = lax.broadcasted_iota(jnp.int32, (FRM, 128), 1)
         high_a, high_b = sum_a.astype(BF16).astype(F32), sum_b.astype(BF16).astype(F32)
         packed = jnp.where(lane_id == 0, high_a, 0.0)
         packed = jnp.where(lane_id == 1, sum_a - high_a, packed)
         packed = jnp.where(lane_id == 2, high_b, packed)
-        packed = jnp.where(lane_id == 3, sum_b - high_b, packed).astype(BF16)
-        for b in range(NX):
-            MS[s, b, :, DX:] = packed
-        for j, xx in xs_:
-            rcopy(MS.at[s, xx], MR.at[s, x], xb_s.at[s, j], xb_r.at[s, x], dev(xx=xx)).start()
-
+        MT[par, x] = jnp.where(lane_id == 3, sum_b - high_b, packed).astype(BF16)
+        for j, xx in far_first:
+            rcopy(MT.at[par, x], MT.at[par, x], xt_s.at[s, j], xt_r.at[s, x], dev(xx=xx)).start()
+
+        pump_back(s, 1)
         for tile in range(lanes_x):
             lane = slice(tile * 128, (tile + 1) * 128)
             spread = SP[16 : 16 + FRM, lane]
@@ -423,130 +599,56 @@
                     spread * GL[s, start : start + FRM, lane] * MASK[k], axis=0, keepdims=True
                 )
 
-        @pl.when((par != c) & (step > 0))
+        @pl.when(((par != c) & (step > 0)) | ((s == 0) & (c == 0)))
         def _():
-            weight_gradient(s + 1)
-
+            ready = jnp.where(par != c, s + 1, 0)
+            weight_gradient(ready)
+            each(scatters, lambda g: g.begin(2, ready // 2))
+
+        pump_back(s, 2)
         for j, xx in xs_:
-            rcopy(MS.at[s, xx], MR.at[s, xx], xb_s.at[s, j], xb_r.at[s, xx], dev(xx=xx)).wait()
-        total = PF[x]
+            rcopy(MS.at[xx], MR.at[par, xx], xb_s.at[s, j], xb_r.at[s, xx], dev(xx=xx)).wait()
+            rcopy(MT.at[par, xx], MT.at[par, xx], xt_s.at[s, j], xt_r.at[s, xx], dev(xx=xx)).wait()
+        total = PF[...]
         for j, xx in xs_:
-            total = total + MR[s, xx, :, :DX].astype(F32)
-            packed = MR[s, xx, :, DX:].astype(F32)
+            total = total + MR[par, xx].astype(F32)
+            packed = MT[par, xx].astype(F32)
             sum_a = sum_a + packed[:, 0:1] + packed[:, 1:2]
             sum_b = sum_b + packed[:, 2:3] + packed[:, 3:4]
-        xhat = (X[s, x].astype(F32) - mean) * inverse
+        xhat = XH[x]
         TT[s, KT : KT + 1, :] = jnp.sum(total * xhat, axis=0, keepdims=True)
         gain = GAIN[par, i, 0:1, cols(x)]
         grad_in = inverse * (total * gain - sum_a * (1.0 / D) - xhat * (sum_b * (1.0 / D)))
         GC[...] = (GC[...] + grad_in).astype(BF16).astype(F32)
+        pump_back(s, 3)
         return 0
 
     lax.fori_loop(0, SECT, backward, 0)
-
-    pl.when(c == 0)(lambda: weight_gradient(0))
 
     for i in range(NX):
         rcopy(TT.at[2 * i + 1 - c], TS.at[i], tt_s.at[4, i], tt_r.at[4, i], sib).start()
 
-    def scatter(cc):
-        n1, n2 = (NY, NZ) if cc == 0 else (NZ, NY)
-        me1, me2 = (y, z) if cc == 0 else (z, y)
-        dirs = ((0, 1), (1, -1))
-
-        def region(i, j, h):
-            return G.at[i, :, j, :, half(h)] if cc == 0 else G.at[i, j, :, :, half(h)]
-
-        def region_value(i, j, h):
-            return G[i, :, j, :, half(h)] if cc == 0 else G[i, j, :, :, half(h)]
-
-        def neighbour(phase, sgn):
-            me, n = (me2, n2) if phase == 0 else (me1, n1)
-            pos = (me + sgn + n) % n
-            along_z = (phase == 0) == (cc == 0)
-            return dev(zz=pos) if along_z else dev(yy=pos)
-
-        def slot_a(i, h, t):
-            return RA.at[i, h, pl.ds((t - 1) * n1, n1)]
-
-        def send_a(i, h, sgn, src, t):
-            return rcopy(src, slot_a(i, h, t), rs_s.at[0, i, h], rs_r.at[0, i, h, t - 1], neighbour(0, sgn))
-
-        def loop(f):
-            lax.fori_loop(0, NX, lambda i, _: (f(i), 0)[1], 0)
-
-        def first_a(i):
-            for h, sgn in dirs:
-                send_a(i, h, sgn, region(i, (me2 - sgn + n2) % n2, h), 1).start()
-
-        loop(first_a)
-
-        def add_a(i, h, sgn, t):
-            send_a(i, h, sgn, slot_a(i, h, t), t).wait_recv()
-            target = (me2 - sgn * (t + 1) + 2 * n2) % n2
-            held = pl.ds((t - 1) * n1, n1)
-            RA[i, h, held] = (RA[i, h, held].astype(F32) + region_value(i, target, h).astype(F32)).astype(BF16)
-
-        def step_a(t, _):
-            def one(i):
-                for h, sgn in dirs:
-                    add_a(i, h, sgn, t)
-                    send_a(i, h, sgn, slot_a(i, h, t), t + 1).start()
-
-            loop(one)
-            return 0
-
-        lax.fori_loop(1, n2 - 1, step_a, 0)
-
-        base = (n2 - 2) * n1
-
-        def send_b(i, h, sgn, src, t):
-            return rcopy(src, RB.at[i, h, t - 1], rs_s.at[1, i, h], rs_r.at[1, i, h, t - 1], neighbour(1, sgn))
-
-        def last_a(i):
-            for h, sgn in dirs:
-                add_a(i, h, sgn, n2 - 1)
-                send_b(i, h, sgn, RA.at[i, h, base + (me1 - sgn + n1) % n1], 1).start()
-
-        loop(last_a)
-
-        def add_b(i, h, sgn, t):
-            send_b(i, h, sgn, RB.at[i, h, t - 1], t).wait_recv()
-            target = (me1 - sgn * (t + 1) + 2 * n1) % n1
-            return RB[i, h, t - 1].astype(F32) + RA[i, h, base + target].astype(F32)
-
-        def step_b(t, _):
-            def one(i):
-                for h, sgn in dirs:
-                    RB[i, h, t - 1] = add_b(i, h, sgn, t).astype(BF16)
-                    send_b(i, h, sgn, RB.at[i, h, t - 1], t + 1).start()
-
-            loop(one)
-            return 0
-
-        lax.fori_loop(1, n1 - 1, step_b, 0)
-
-        def last_b(i):
-            for h, sgn in dirs:
-                FS[i, :, half(h)] = add_b(i, h, sgn, n1 - 1).astype(BF16)
-
-        loop(last_b)
-
-        def drain(i, _):
-            for h in range(2):
-                sent_a, sent_b = RA.at[i, h, 0 : (n2 - 1) * n1], RB.at[i, h, 0 : n1 - 1]
-                rcopy(sent_a, sent_a, rs_s.at[0, i, h], rs_r.at[0, i, h, 0], sib).wait_send()
-                rcopy(sent_b, sent_b, rs_s.at[1, i, h], rs_r.at[1, i, h, 0], sib).wait_send()
-            return 0
-
-        lax.fori_loop(0, NX, drain, 0)
-
-    for cc in range(CORES):
-        pl.when(c == cc)(functools.partial(scatter, cc))
-
-    for j, xx in xs_:
-        rcopy(FS.at[xx], FR.at[x], fin_s.at[j], fin_r.at[x], dev(xx=xx)).start()
-    FR[x] = FS[x]
+    def rest(g):
+        if g.cc == 0 and NX > 1:
+            for e in range(5, 2 * g.h2):
+                g.step(2, *at(e), 1)
+        for i in range(1, NX):
+            g.begin(1, i)
+
+    def tail(low, high, g):
+        for e in range(low, high):
+            if e < 2 * g.h2:
+                g.step(2, *at(e), 0)
+            if e < 2 * g.h1:
+                for i in range(1, NX):
+                    g.step(1, *at(e), i)
+            if e == 2 * g.h2 - 1:
+                g.begin(1, 0)
+            if 0 <= e - 2 * g.h2 < 2 * g.h1:
+                g.step(1, *at(e - 2 * g.h2), 0)
+
+    each(scatters, rest)
+    each(scatters, functools.partial(tail, 0, 2))
 
     for i in range(NX):
         rcopy(TT.at[2 * i + 1 - c], TS.at[i], tt_s.at[4, i], tt_r.at[4, i], sib).wait()
@@ -558,18 +660,21 @@
     for j, yy in ys_:
         rcopy(TY.at[yy], TYR.at[y], tt_s.at[0, j], tt_r.at[0, y], dev(yy=yy)).start()
     TYR[y] = TY[y]
+    each(scatters, functools.partial(tail, 2, 4))
     for j, yy in ys_:
         rcopy(TY.at[yy], TYR.at[yy], tt_s.at[0, j], tt_r.at[0, yy], dev(yy=yy)).wait()
     TY[y] = sum(TYR[k] for k in range(NY))
     for j, zz in zs_:
         rcopy(TY.at[y, zz], TZR.at[z], tt_s.at[1, j], tt_r.at[1, z], dev(zz=zz)).start()
     TZR[z] = TY[y, z]
+    each(scatters, functools.partial(tail, 4, 6))
     for j, zz in zs_:
         rcopy(TY.at[y, zz], TZR.at[zz], tt_s.at[1, j], tt_r.at[1, zz], dev(zz=zz)).wait()
     TX[...] = sum(TZR[k] for k in range(NZ))
     for j, xx in xs_:
         rcopy(TX, TXR.at[x], tt_s.at[2, j], tt_r.at[2, x], dev(xx=xx)).start()
     TXR[x] = TX[...]
+    each(scatters, functools.partial(tail, 6, 8))
     for j, xx in xs_:
         rcopy(TX, TXR.at[xx], tt_s.at[2, j], tt_r.at[2, xx], dev(xx=xx)).wait()
     TO1[z] = jnp.zeros(TO1.shape[1:], F32)
@@ -581,11 +686,16 @@
             TO1[z, k : k + 1, :] = row[:, tile * 128 : (tile + 1) * 128]
     for j, zz in zs_:
         rcopy(TO1.at[z], TO1.at[z], tt_s.at[3, j], tt_r.at[3, z], dev(zz=zz)).start()
+    each(scatters, functools.partial(tail, 8, 10))
     for j, zz in zs_:
         rcopy(TO1.at[z], TO1.at[zz], tt_s.at[3, j], tt_r.at[3, zz], dev(zz=zz)).wait()
     for j, yy in ys_:
         rcopy(TO1, TO2.at[y], tt_s.at[5, j], tt_r.at[5, y], dev(yy=yy)).start()
     TO2[y] = TO1[...]
+    each(scatters, functools.partial(tail, 10, 12))
+    for j, xx in xs_:
+        rcopy(FS.at[xx], FR.at[x], fin_s.at[j], fin_r.at[x], dev(xx=xx)).start()
+    FR[x] = FS[x]
     for j, yy in ys_:
         rcopy(TO1, TO2.at[yy], tt_s.at[5, j], tt_r.at[5, yy], dev(yy=yy)).wait()
     o_taps[...] = TO2[...].reshape(o_taps.shape)
@@ -607,6 +717,8 @@
         return 0
 
     lax.fori_loop(0, NX, drain, 0)
+    each(gathers, lambda g: g.drain())
+    each(scatters, lambda g: g.drain())
 
 
 def body(
@@ -649,8 +761,9 @@
     tg = jnp.concatenate([conv_taps[0], norm_gain], axis=0)
     gain8 = jnp.broadcast_to(norm_gain, (8, D))
     sub = jnp.pad(subsample_weight, ((0, J * 128 - feats), (0, 0)))
+    sub = sub.reshape(J * 128, NX // 2, 2 * DX).transpose(1, 0, 2).reshape(NX // 2, NZ, R, 2 * DX)
     OR = -(-(D // 128) // 8) * 8
-    NR = max(NY, NZ) - 1
+    NR = max(NY, NZ) // 2
 
     def vm(shape, kind=F32):
         return pltpu.VMEM(shape, kind)
@@ -677,14 +790,17 @@
         vm((SECT, FRM, DX)),
         vm((SECT, FRM, DX)),
         vm((FRM, DX)),
+        vm((FRM, DX), BF16),
+        vm((FRM, DX)),
         vm((NX, FRM, DX)),
         vm((SECT, FRM, 2 * DX), BF16),
         vm((NX, FRM, 2 * DX), BF16),
-        vm((SECT, NX, FRM, DX + 128), BF16),
-        vm((SECT, NX, FRM, DX + 128), BF16),
+        vm((NX, FRM, DX), BF16),
+        vm((2, NX, FRM, DX), BF16),
+        vm((2, NX, FRM, 128), BF16),
         vm((NX, NY, NZ, R, 2 * DX), BF16),
-        vm((NX, 2, max((NZ - 1) * NY, (NY - 1) * NZ), R, DX), BF16),
-        vm((NX, 2, NR, R, DX), BF16),
+        vm((NX, 2, ND // 2, R, 2 * DX), BF16),
+        vm((NX, 2, NR, R, 2 * DX), BF16),
         vm((NX, R, 2 * DX), BF16),
         vm((NX, R, 2 * DX), BF16),
         vm((SECT, KT + 1, DX)),
@@ -696,21 +812,27 @@
         vm((NX, 8, DX)),
         vm((NZ, OR, 128)),
         vm((NY, NZ, OR, 128)),
-        sems(2),
+        sems(4),
         sems(NX),
         sems(NX),
         sems(2, NX),
         sems(2, NX),
         sems(2, max(NY, NZ)),
         sems(2, max(NY, NZ)),
-        sems(2, NX, 2),
-        sems(2, NX, 2, NR),
-        sems(2, NX, 2),
-        sems(2, NX, 2, NR),
+        sems(NX, 2, 2),
+        sems(NX, 2, 2, NR),
+        sems(NX, 2, 2),
+        sems(NX, 2, 2, NR),
+        sems(NX, 2, 2),
+        sems(NX, 2, 2, NR),
+        sems(NX, 2, 2),
+        sems(NX, 2, 2, NR),
         sems(NX),
         sems(NX),
         sems(2),
         sems(2),
+        sems(SECT, NX),
+        sems(SECT, NX),
         sems(SECT, NX),
         sems(SECT, NX),
         sems(SECT, NX),
@@ -733,7 +855,7 @@
             jax.ShapeDtypeStruct((1, R, D), F32),
             jax.ShapeDtypeStruct((ND, OR, 128), F32),
         ),
-        in_specs=[in_vmem, in_any, in_any, in_vmem, in_vmem, in_vmem, in_vmem],
+        in_specs=[in_vmem, in_any, in_any, in_vmem, in_vmem, in_any, in_any],
         out_specs=(in_vmem, in_vmem, in_vmem),
         scratch_shapes=scratch,
         compiler_params=pltpu.CompilerParams(

time: 291 us -> 242 us (0.83)
  Pallas kernels: 277 us -> 230 us
    pallas_call x1, Pallas kernels: 277 us -> 230 us  [body(): pl.pallas_call(functools.partial(kernel, dims), out_shape=(jax.ShapeDtype...]
where the time goes in v2:
time: 242 us
  Pallas kernels  230 us (95%)
  local copies, waits for them, and re-layouts  8.18 us (3%)
    pallas_call x1, Pallas kernels, body(): pl.pallas_call(functools.partial(kernel, dims), out_shape=(jax.ShapeDtype...  230 us

profile of v2, /device:TPU:8, one launch (start us, length us, event | category | flops | bytes accessed | tf_op | source)
XLA Modules:
  0.0 241.8 jit_solution(18067813312820216266)
XLA Ops:
  0.6 0.0 copy-start
  0.6 0.8 convert_bitcast_fusion
  1.4 0.7 convert_bitcast_fusion.2
  2.1 0.1 copy.22
  2.2 0.9 pad.12
  3.1 0.8 fusion
  4.0 0.7 copy.25
  4.6 0.0 copy-done
  4.6 0.1 pad.14
  4.7 0.0 copy-start.3
  4.7 0.0 copy-start.4
  4.7 1.1 copy.30
  5.8 0.0 copy-done.3
  5.9 0.0 copy-done.4
  5.9 0.7 pad_maximum_fusion.tg
  6.6 0.6 broadcast_in_dim.13.gain8
  7.2 229.9 %shard_map.138 = (f32[1,48,1536]{2,1,0:T(8,128)}, f32[1,48,1536]{2,1,0:T(8,128)}, f32[32,16,128]{2,1,0:T(8,128)}) custom-call(bf16[32,16,128]{2,1,0:T(8,128)(2,1)} %bitcast.29, bf16[1,48,1536]{2,1,0:T(8,128)(2,1)} %mixing.1, bf16[1,48,1536]{2,1,0:T(8,128)(2,1)} %gating.1, f32[32,1536]{1,0:T(8,128)} %pad_maximum_fusion.tg, f32[8,1536]{1,0:T(8,128)} %broadcast_in_dim.13.gain8, ...), custom_call_target="tpu_custom_call" | custom-call | tf_op jit(solution)/shard_map/pallas_call | solution.py:851
  237.1 0.0 copy-start.2
  237.1 0.0 copy-start.1
  237.1 1.0 slice.13
  238.2 0.9 broadcast_in_dim.15
  239.0 0.7 slice_bitcast_fusion
  239.7 0.6 copy.32
  240.3 0.0 copy-done.2
  240.3 0.7 copy.35
  241.0 0.0 copy-done.1
  241.0 0.7 copy.36
  (4 shorter events, 0.1 us)
Async XLA Ops:
  0.6 4.0 %copy-start = (bf16[320,1536]{1,0:T(8,128)(2,1)S(1)}, bf16[320,1536]{1,0:T(8,128)(2,1)}, u32[]{:S(2)}) copy-start(bf16[320,1536]{1,0:T(8,128)(2,1)} %param.16) | copy-start | bytes 2949124
  4.7 1.1 copy-start.3
  4.7 1.1 copy-start.4
  237.1 3.2 %copy-start.2 = (f32[1,48,1536]{2,1,0:T(8,128)S(1)}, f32[1,48,1536]{2,1,0:T(8,128)}, u32[]{:S(2)}) copy-start(f32[1,48,1536]{2,1,0:T(8,128)} %get-tuple-element.24) | copy-start | bytes 884740
  237.1 3.9 %copy-start.1 = (f32[1,48,1536]{2,1,0:T(8,128)S(1)}, f32[1,48,1536]{2,1,0:T(8,128)}, u32[]{:S(2)}) copy-start(f32[1,48,1536]{2,1,0:T(8,128)} %get-tuple-element.25) | copy-start | bytes 884740

commit v3 on v2

--- a/solution.py
+++ b/solution.py
@@ -28,19 +28,28 @@
 
 def kernel(
     dims,
-    slabs,
+    mel,
+    ids,
+    lengths,
+    shards,
+    slots,
     mixing,
     gating,
-    tg,
-    gain8,
+    taps_in,
+    gain_in,
     sub,
     cot,
     o_mix,
     o_gate,
     o_taps,
+    o_gain,
     W,
     TAPS,
     GAIN,
+    tg,
+    gain8,
+    MF,
+    slabs,
     T1,
     T2,
     TF,
@@ -157,18 +166,46 @@
         rcopy(mixing.at[0, :, cols(xx)], W.at[c, x, y, z, :, half(0)], xw_s.at[j], xw_r.at[x], dev(xx=xx)).start()
         rcopy(gating.at[0, :, cols(xx)], W.at[c, x, y, z, :, half(1)], xw_s.at[j], xw_r.at[x], dev(xx=xx)).start()
     own_copies = [
-        pltpu.make_async_copy(sub, G.at[0, 0 : NX // 2], lw_s.at[2]),
-        pltpu.make_async_copy(cot.at[pl.ds(pl.multiple_of(c * FRM, 16), FRM), cols(x)], CT, lw_s.at[3]),
+        pltpu.make_async_copy(cot.at[pl.ds(pl.multiple_of(c * FRM, 16), FRM), cols(x)], CT, lw_s.at[2]),
         pltpu.make_async_copy(mixing.at[0, :, cols(x)], W.at[c, x, y, z, :, half(0)], lw_s.at[0]),
         pltpu.make_async_copy(gating.at[0, :, cols(x)], W.at[c, x, y, z, :, half(1)], lw_s.at[1]),
     ]
+    feats = sub.shape[0]
+    for k in range(NX // 2):
+        for b in range(NZ):
+            count = max(0, min(feats - b * R, R))
+            if count < R:
+                G[0, k, b, count:] = jnp.zeros((R - count, 2 * DX), BF16)
+            if count > 0:
+                part = sub.at[b * R : b * R + count, k * 2 * DX : (k + 1) * 2 * DX]
+                own_copies.append(pltpu.make_async_copy(part, G.at[0, k, b, 0:count], lw_s.at[3 + k * NZ + b]))
     for copy in own_copies:
         copy.start()
+
+    MF[...] = mel[...].astype(F32)
+    order = shards[...] == lax.broadcasted_iota(jnp.int32, (ND, ND), 0)
+    order_bf = order.astype(F32).astype(BF16)
+    TF[...] = jnp.zeros(TF.shape, F32)
+    for f in range(TSUB):
+        moved = jnp.dot(order_bf, MF[:, f, :].astype(BF16), preferred_element_type=F32)
+        for j in range(J):
+            wide = min(128, feats - j * 128)
+            TF[:, f * J + j, :wide] = moved[:, j * 128 : j * 128 + wide]
+    lane_of = lax.broadcasted_iota(jnp.int32, (ND, 128), 1)
+    details = jnp.zeros((ND, 128), F32)
+    for k, row in enumerate((slots, ids, lengths)):
+        column = jnp.sum(jnp.where(order, row[...].astype(F32), 0.0), axis=1, keepdims=True)
+        details = jnp.where(lane_of == k, column, details)
+    TF[:, TSUB * J, :] = details
+    slabs[...] = TF[...].astype(BF16)
 
     for j, yy in ys_:
         rcopy(slabs.at[pl.ds(yy * NZ, NZ)], T1.at[y], tl_s.at[0, j], tl_r.at[0, y], dev(yy=yy)).start()
     T1[y] = slabs[pl.ds(y * NZ, NZ)]
 
+    tg[0:KT] = taps_in[0]
+    tg[KT : KT + 1] = gain_in[...]
+    gain8[...] = jnp.broadcast_to(gain_in[...], gain8.shape)
     for j, xx in xs_:
         rcopy(tg.at[:, cols(xx)], TAPS.at[c, x], tg_s.at[0, j], tg_r.at[0, x], dev(xx=xx)).start()
         rcopy(gain8, GAIN.at[c, x], tg_s.at[1, j], tg_r.at[1, x], dev(xx=xx)).start()
@@ -267,7 +304,6 @@
             lax.fori_loop(0, NX, one, 0)
 
     gathers = [Gather(cc) for cc in range(CORES)]
-    most = max(NY, NZ)
 
     def each(rings, f):
         for cc in range(CORES):
@@ -278,7 +314,7 @@
         for e in range(2 * g.h1):
             g.step(1, *at(e), 0)
         g.begin(2, 0)
-        for i in range(1, NX):
+        for i in range(1, NX if g.cc == 0 else min(NX, 2)):
             g.begin(1, i)
 
     def go_on(low, high, g):
@@ -286,10 +322,16 @@
             if e < 2 * g.h2:
                 g.step(2, *at(e), 0)
             if e < 2 * g.h1:
-                for i in range(1, NX):
+                for i in range(1, NX if g.cc == 0 else min(NX, 2)):
                     g.step(1, *at(e), i)
             if e == 2 * g.h1 - 1 and NX > 1:
                 g.begin(2, 1)
+                if g.cc == 1 and NX > 2:
+                    g.begin(1, 2)
+            if g.cc == 0 and 0 <= e - 4 < 2 * g.h2 and NX > 1:
+                g.step(2, *at(e - 4), 1)
+        if g.cc == 0 and high == 8 and NX > 2:
+            g.begin(2, 2)
 
     each(gathers, begin)
 
@@ -348,25 +390,37 @@
         return 0
 
     lax.fori_loop(0, SECT, clear, 0)
-    each(gathers, functools.partial(go_on, 3, most))
+    each(gathers, functools.partial(go_on, 3, 8))
 
     rcopy(TAPS.at[1 - c], TAPS.at[1 - c], st_s.at[0], st_r.at[0], sib).wait_recv()
     rcopy(GAIN.at[1 - c], GAIN.at[1 - c], st_s.at[1], st_r.at[1], sib).wait_recv()
 
     def pump(s, q):
         pair = s // 2 + 1
-
-        def one(g):
-            if g.cc == 0:
-                t, u, e = 1 + (s % 2) * 2 + q // 2, q % 2, (s % 2) * 4 + q
-            elif q % 2 == 0:
-                t, u, e = 1 + s % 2, q // 2, (s % 2) * 2 + q // 2
+        u = q // 2
+
+        def run(g, ring, t, u, i):
+            pl.when((i < NX) & (t <= (g.h1 if ring == 1 else g.h2)))(lambda: g.step(ring, t, u, i))
+
+        def first(g):
+            if q % 2 == 0:
+                run(g, 2, 3 + s % 2, u, pair)
             else:
-                return
-            pl.when((pair < NX) & (t <= g.h2))(lambda: g.step(2, t, u, pair))
-            pl.when((pair + 1 < NX) & (e == max(2 * g.h2 - 3, 0)))(lambda: g.begin(2, pair + 1))
-
-        each(gathers, one)
+                run(g, 2, 1 + s % 2, u, pair + 1)
+            if q == 3:
+                pl.when((s % 2 == 1) & (pair + 2 < NX))(lambda: g.begin(2, pair + 2))
+
+        def second(g):
+            if q % 2 == 0:
+                run(g, 2, 1 + s % 2, u, pair)
+            else:
+                for part in range(2):
+                    run(g, 1, 1 + (s % 2) * 2 + u, part, pair + 1)
+            if q == 3:
+                pl.when((s % 2 == 1) & (pair + 1 < NX))(lambda: g.begin(2, pair + 1))
+                pl.when((s % 2 == 1) & (pair + 2 < NX))(lambda: g.begin(1, pair + 2))
+
+        each(gathers, lambda g: first(g) if g.cc == 0 else second(g))
 
     def statistics(s):
         blocks = [X[s, b].astype(F32) for b in range(NX)]
@@ -523,20 +577,43 @@
 
     scatters = [Scatter(cc) for cc in range(CORES)]
 
+    both_parts = (0, 1)
+    plan = {
+        (0, 0): {0: [(2, 3, (1,), 1)], 1: [(2, 4, (0,), 1)], 2: [(2, 4, (1,), 1)], 3: [(2, 1, (0,), 0), (1, 0, None, 1)]},
+        (0, 1): {
+            0: [(2, 1, (1,), 1), (1, 1, both_parts, 2)],
+            1: [(2, 2, (0,), 1)],
+            2: [(2, 2, (1,), 1), (1, 2, both_parts, 2)],
+            3: [(2, 3, (0,), 1)],
+        },
+        (1, 0): {
+            0: [(2, 1, (0,), 0)],
+            1: [(1, 1, both_parts, 1)],
+            2: [(2, 1, (1,), 0)],
+            3: [(1, 2, both_parts, 1)],
+        },
+        (1, 1): {
+            0: [(2, 2, (0,), 1)],
+            1: [(1, 3, both_parts, 2)],
+            2: [(2, 2, (1,), 1)],
+            3: [(1, 4, both_parts, 2), (1, 0, None, 1)],
+        },
+    }
+
     def pump_back(s, q):
-        k = s // 2
-
         def one(g):
-            if g.cc == 0:
-                odd = {0: (5, 2), 1: (6, 2), 2: (7, 2), 3: (0, 1)}[q]
-                even = (1 + q, 1)
-            else:
-                odd = {0: (0, 1), 2: (1, 1)}.get(q)
-                even = {0: (2, 1), 2: (3, 1)}.get(q)
-            for parity, what in ((1, odd), (0, even)):
-                if what is not None and what[0] < 2 * g.h2:
-                    e, ahead = what
-                    pl.when((s % 2 == parity) & (k + ahead < NX))(lambda: g.step(2, *at(e), k + ahead))
+            for parity in range(2):
+                for ring, t, parts, ahead in plan[g.cc, parity][q]:
+                    if t <= (g.h1 if ring == 1 else g.h2):
+                        pair = s // 2 + ahead
+
+                        @pl.when((s % 2 == parity) & (pair < NX))
+                        def _():
+                            if t == 0:
+                                g.begin(ring, pair)
+                            else:
+                                for u in parts:
+                                    g.step(ring, t, u, pair)
 
         each(scatters, one)
 
@@ -599,11 +676,10 @@
                     spread * GL[s, start : start + FRM, lane] * MASK[k], axis=0, keepdims=True
                 )
 
-        @pl.when(((par != c) & (step > 0)) | ((s == 0) & (c == 0)))
+        @pl.when(par == c)
         def _():
-            ready = jnp.where(par != c, s + 1, 0)
-            weight_gradient(ready)
-            each(scatters, lambda g: g.begin(2, ready // 2))
+            weight_gradient(s)
+            each(scatters, lambda g: g.begin(2, i))
 
         pump_back(s, 2)
         for j, xx in xs_:
@@ -628,26 +704,18 @@
     for i in range(NX):
         rcopy(TT.at[2 * i + 1 - c], TS.at[i], tt_s.at[4, i], tt_r.at[4, i], sib).start()
 
-    def rest(g):
-        if g.cc == 0 and NX > 1:
-            for e in range(5, 2 * g.h2):
-                g.step(2, *at(e), 1)
-        for i in range(1, NX):
-            g.begin(1, i)
-
     def tail(low, high, g):
+        done = 1 if g.cc == 0 else 2
         for e in range(low, high):
-            if e < 2 * g.h2:
+            if done <= e < 2 * g.h2:
                 g.step(2, *at(e), 0)
-            if e < 2 * g.h1:
-                for i in range(1, NX):
-                    g.step(1, *at(e), i)
+            if NX > 1 and e < 2 * g.h1 and (g.cc == 0 or e >= 4):
+                g.step(1, *at(e), 1)
             if e == 2 * g.h2 - 1:
                 g.begin(1, 0)
             if 0 <= e - 2 * g.h2 < 2 * g.h1:
                 g.step(1, *at(e - 2 * g.h2), 0)
 
-    each(scatters, rest)
     each(scatters, functools.partial(tail, 0, 2))
 
     for i in range(NX):
@@ -698,7 +766,14 @@
     FR[x] = FS[x]
     for j, yy in ys_:
         rcopy(TO1, TO2.at[yy], tt_s.at[5, j], tt_r.at[5, yy], dev(yy=yy)).wait()
-    o_taps[...] = TO2[...].reshape(o_taps.shape)
+    for k in range(D // 128):
+        lane = slice(k * 128, (k + 1) * 128)
+        for yy in range(NY):
+            low, count = yy * NZ, min(NZ, KT - yy * NZ)
+            piece = TO2[yy, :, k, :]
+            o_taps[0, low : low + count, lane] = piece[:count]
+            if count < NZ:
+                o_gain[:, lane] = piece[count : count + 1]
 
     for j, xx in xs_:
         rcopy(FS.at[xx], FR.at[xx], fin_s.at[j], fin_r.at[xx], dev(xx=xx)).wait()
@@ -748,20 +823,6 @@
     SR = -(-(TSUB * J + 1) // 16) * 16
     dims = dict(X=NX, Y=NY, Z=NZ, D=D, R=R, F=FRM, TSUB=TSUB, J=J, TAPS=KT)
 
-    details = jnp.stack([dest_slot, utt_ids, tile_lengths], axis=1).astype(BF16)
-    flat = jnp.concatenate(
-        [
-            jnp.pad(mel_tiles, ((0, 0), (0, 0), (0, J * 128 - feats))).reshape(tiles, TSUB * J * 128),
-            jnp.pad(details, ((0, 0), (0, 125 + (SR - TSUB * J - 1) * 128))),
-        ],
-        axis=1,
-    )
-    order = (dest_shard[None, :] == jnp.arange(ND, dtype=jnp.int32)[:, None]).astype(BF16)
-    slabs = jnp.dot(order, flat, preferred_element_type=F32).astype(BF16).reshape(ND, SR, 128)
-    tg = jnp.concatenate([conv_taps[0], norm_gain], axis=0)
-    gain8 = jnp.broadcast_to(norm_gain, (8, D))
-    sub = jnp.pad(subsample_weight, ((0, J * 128 - feats), (0, 0)))
-    sub = sub.reshape(J * 128, NX // 2, 2 * DX).transpose(1, 0, 2).reshape(NX // 2, NZ, R, 2 * DX)
     OR = -(-(D // 128) // 8) * 8
     NR = max(NY, NZ) // 2
 
@@ -775,6 +836,10 @@
         vm((2, NX, NY, NZ, R, 2 * DX), BF16),
         vm((2, NX, KT + 1, DX)),
         vm((2, NX, 8, D)),
+        vm((KT + 1, D)),
+        vm((8, D)),
+        vm((tiles, TSUB, feats)),
+        vm((ND, SR, 128), BF16),
         vm((NY, NZ, SR, 128), BF16),
         vm((NZ, NY, SR, 128), BF16),
         vm((ND, SR, 128)),
@@ -812,7 +877,7 @@
         vm((NX, 8, DX)),
         vm((NZ, OR, 128)),
         vm((NY, NZ, OR, 128)),
-        sems(4),
+        sems(3 + NX * NZ),
         sems(NX),
         sems(NX),
         sems(2, NX),
@@ -848,22 +913,33 @@
     ]
     in_vmem = pl.BlockSpec(memory_space=pltpu.VMEM)
     in_any = pl.BlockSpec(memory_space=pl.ANY)
-    mix, gate, taps = pl.pallas_call(
+    return pl.pallas_call(
         functools.partial(kernel, dims),
         out_shape=(
             jax.ShapeDtypeStruct((1, R, D), F32),
             jax.ShapeDtypeStruct((1, R, D), F32),
-            jax.ShapeDtypeStruct((ND, OR, 128), F32),
+            jax.ShapeDtypeStruct((1, KT, D), F32),
+            jax.ShapeDtypeStruct((1, D), F32),
         ),
-        in_specs=[in_vmem, in_any, in_any, in_vmem, in_vmem, in_any, in_any],
-        out_specs=(in_vmem, in_vmem, in_vmem),
+        in_specs=[in_vmem] * 5 + [in_any] * 2 + [in_vmem] * 2 + [in_any] * 2,
+        out_specs=(in_vmem,) * 4,
         scratch_shapes=scratch,
         compiler_params=pltpu.CompilerParams(
             collective_id=0, has_side_effects=True, vmem_limit_bytes=VMEM_LIMIT
         ),
-    )(slabs, mixing_weight, gate_weight, tg, gain8, sub, out_cot)
-    rows = taps[:, : D // 128].reshape(ND, D)
-    return mix, gate, rows[None, :KT], rows[KT:]
+    )(
+        mel_tiles,
+        utt_ids[None],
+        tile_lengths[None],
+        dest_shard[None],
+        dest_slot[None],
+        mixing_weight,
+        gate_weight,
+        conv_taps,
+        norm_gain,
+        subsample_weight,
+        out_cot,
+    )
 
 
 def solution(mesh):

time: 242 us -> 228 us (0.942)
  Pallas kernels: 230 us -> 221 us
    pallas_call x1, Pallas kernels: 230 us -> 221 us  [body(): pl.pallas_call(functools.partial(kernel, dims), out_shape=(jax.ShapeDtype...]
where the time goes in v3:
time: 228 us; the launch traced here: 227 us
  Pallas kernels  221 us (97%)
  local copies, waits for them, and re-layouts  5.84 us (3%)
    pallas_call x1, Pallas kernels, body(): pl.pallas_call(functools.partial(kernel, dims), out_shape=(jax.ShapeDtype...  221 us

profile of v3, /device:TPU:8, one launch (start us, length us, event | category | flops | bytes accessed | tf_op | source)
XLA Modules:
  0.0 227.4 jit_solution(8012137847026486822)
XLA Ops:
  0.6 1.6 copy.15.taps_in
  2.2 220.9 %shard_map.138 = (f32[1,48,1536]{2,1,0:T(8,128)}, f32[1,48,1536]{2,1,0:T(8,128)}, f32[1,31,1536]{2,1,0:T(8,128)}, f32[1,1536]{1,0:T(1,128)}) custom-call(bf16[32,4,320]{2,1,0:T(4,128)(2,1)} %mel.1, s32[1,32]{1,0:T(1,128)} %bitcast.4, s32[1,32]{1,0:T(1,128)} %bitcast.5, s32[1,32]{1,0:T(1,128)} %bitcast.6, s32[1,32]{1,0:T(1,128)} %bitcast.7, ...), custom_call_target="tpu_custom_call" | custom-call | tf_op jit(solution)/shard_map/pallas_call | solution.py:916
  223.2 0.0 copy-start.1
  223.2 1.8 copy.16
  225.0 0.0 copy-done.1
  225.0 0.0 copy-start
  225.0 0.7 copy.20
  225.7 0.4 copy-done
  226.1 0.0 copy-start.2
  226.1 0.7 copy.21
  226.8 0.0 copy-done.2
  226.8 0.6 copy.22
Async XLA Ops:
  223.2 1.9 copy-start.1
  225.0 1.1 copy-start
  226.1 0.7 copy-start.2

commit v4 on v3

--- a/solution.py
+++ b/solution.py
@@ -310,25 +310,36 @@
             pl.when(c == cc)(functools.partial(f, rings[cc]))
 
     def begin(g):
+        if g.cc == 1:
+            for i in range(NX):
+                g.begin(1, i)
+            for e in range(2 * g.h1):
+                for i in range(NX):
+                    g.step(1, *at(e), i)
+                    if e == 2 * g.h1 - 1 and i == 0:
+                        g.begin(2, 0)
+            return
         g.begin(1, 0)
         for e in range(2 * g.h1):
             g.step(1, *at(e), 0)
         g.begin(2, 0)
-        for i in range(1, NX if g.cc == 0 else min(NX, 2)):
+        for i in range(1, NX):
             g.begin(1, i)
 
     def go_on(low, high, g):
         for e in range(low, high):
             if e < 2 * g.h2:
                 g.step(2, *at(e), 0)
+            if g.cc == 1:
+                if e == 1 and NX > 1:
+                    g.begin(2, 1)
+                continue
             if e < 2 * g.h1:
-                for i in range(1, NX if g.cc == 0 else min(NX, 2)):
+                for i in range(1, NX):
                     g.step(1, *at(e), i)
             if e == 2 * g.h1 - 1 and NX > 1:
                 g.begin(2, 1)
-                if g.cc == 1 and NX > 2:
-                    g.begin(1, 2)
-            if g.cc == 0 and 0 <= e - 4 < 2 * g.h2 and NX > 1:
+            if 0 <= e - 4 < 2 * g.h2 and NX > 1:
                 g.step(2, *at(e - 4), 1)
         if g.cc == 0 and high == 8 and NX > 2:
             g.begin(2, 2)
@@ -399,26 +410,22 @@
         pair = s // 2 + 1
         u = q // 2
 
-        def run(g, ring, t, u, i):
-            pl.when((i < NX) & (t <= (g.h1 if ring == 1 else g.h2)))(lambda: g.step(ring, t, u, i))
+        def run(g, t, u, i):
+            pl.when((i < NX) & (t <= g.h2))(lambda: g.step(2, t, u, i))
 
         def first(g):
             if q % 2 == 0:
-                run(g, 2, 3 + s % 2, u, pair)
+                run(g, 3 + s % 2, u, pair)
             else:
-                run(g, 2, 1 + s % 2, u, pair + 1)
+                run(g, 1 + s % 2, u, pair + 1)
             if q == 3:
                 pl.when((s % 2 == 1) & (pair + 2 < NX))(lambda: g.begin(2, pair + 2))
 
         def second(g):
             if q % 2 == 0:
-                run(g, 2, 1 + s % 2, u, pair)
-            else:
-                for part in range(2):
-                    run(g, 1, 1 + (s % 2) * 2 + u, part, pair + 1)
+                run(g, 1 + s % 2, u, pair)
             if q == 3:
-                pl.when((s % 2 == 1) & (pair + 1 < NX))(lambda: g.begin(2, pair + 1))
-                pl.when((s % 2 == 1) & (pair + 2 < NX))(lambda: g.begin(1, pair + 2))
+                pl.when((s % 2 == 0) & (pair + 1 < NX))(lambda: g.begin(2, pair + 1))
 
         each(gathers, lambda g: first(g) if g.cc == 0 else second(g))
 
@@ -579,12 +586,17 @@
 
     both_parts = (0, 1)
     plan = {
-        (0, 0): {0: [(2, 3, (1,), 1)], 1: [(2, 4, (0,), 1)], 2: [(2, 4, (1,), 1)], 3: [(2, 1, (0,), 0), (1, 0, None, 1)]},
+        (0, 0): {
+            0: [(2, 4, (1,), 2), (1, 0, None, 2)],
+            1: [(2, 2, (1,), 1)],
+            2: [(2, 3, (0,), 1)],
+            3: [(2, 1, (0,), 0)],
+        },
         (0, 1): {
-            0: [(2, 1, (1,), 1), (1, 1, both_parts, 2)],
-            1: [(2, 2, (0,), 1)],
-            2: [(2, 2, (1,), 1), (1, 2, both_parts, 2)],
-            3: [(2, 3, (0,), 1)],
+            0: [(2, 3, (1,), 2), (1, 1, both_parts, 3)],
+            1: [(2, 1, (1,), 1)],
+            2: [(2, 4, (0,), 2), (1, 2, both_parts, 3)],
+            3: [(2, 2, (0,), 1)],
         },
         (1, 0): {
             0: [(2, 1, (0,), 0)],
@@ -667,6 +679,11 @@
             rcopy(MT.at[par, x], MT.at[par, x], xt_s.at[s, j], xt_r.at[s, x], dev(xx=xx)).start()
 
         pump_back(s, 1)
+        @pl.when(par == c)
+        def _():
+            weight_gradient(s)
+            each(scatters, lambda g: g.begin(2, i))
+
         for tile in range(lanes_x):
             lane = slice(tile * 128, (tile + 1) * 128)
             spread = SP[16 : 16 + FRM, lane]
@@ -675,11 +692,6 @@
                 TT[s, k : k + 1, lane] = jnp.sum(
                     spread * GL[s, start : start + FRM, lane] * MASK[k], axis=0, keepdims=True
                 )
-
-        @pl.when(par == c)
-        def _():
-            weight_gradient(s)
-            each(scatters, lambda g: g.begin(2, i))
 
         pump_back(s, 2)
         for j, xx in xs_:
@@ -706,10 +718,20 @@
 
     def tail(low, high, g):
         done = 1 if g.cc == 0 else 2
+        late = {0: 5, 2: 6, 3: 7} if g.cc == 0 and NX > 1 else {}
         for e in range(low, high):
+            if late.get(e, 8) < 2 * g.h2:
+                g.step(2, *at(late[e]), 1)
             if done <= e < 2 * g.h2:
                 g.step(2, *at(e), 0)
-            if NX > 1 and e < 2 * g.h1 and (g.cc == 0 or e >= 4):
+            if g.cc == 0:
+                if NX > 2 and e < 2 * g.h1:
+                    g.step(1, *at(e), 2)
+                if NX > 1 and e == 3:
+                    g.begin(1, 1)
+                if NX > 1 and 0 <= e - 4 < 2 * g.h1:
+                    g.step(1, *at(e - 4), 1)
+            elif NX > 1 and 4 <= e < 2 * g.h1:
                 g.step(1, *at(e), 1)
             if e == 2 * g.h2 - 1:
                 g.begin(1, 0)

time: 228 us -> 206 us (0.904)
  Pallas kernels: 221 us -> 199 us
    pallas_call x1, Pallas kernels: 221 us -> 199 us  [body(): pl.pallas_call(functools.partial(kernel, dims), out_shape=(jax.ShapeDtype...]
where the time goes in v4:
time: 206 us; the launch traced here: 205 us
  Pallas kernels  199 us (97%)
  local copies, waits for them, and re-layouts  5.84 us (3%)
    pallas_call x1, Pallas kernels, body(): pl.pallas_call(functools.partial(kernel, dims), out_shape=(jax.ShapeDtype...  199 us

profile of v4, /device:TPU:8, one launch (start us, length us, event | category | flops | bytes accessed | tf_op | source)
XLA Modules:
  0.0 205.4 jit_solution(13314738391339806809)
XLA Ops:
  0.6 1.6 copy.15.taps_in
  2.2 198.9 %shard_map.138 = (f32[1,48,1536]{2,1,0:T(8,128)}, f32[1,48,1536]{2,1,0:T(8,128)}, f32[1,31,1536]{2,1,0:T(8,128)}, f32[1,1536]{1,0:T(1,128)}) custom-call(bf16[32,4,320]{2,1,0:T(4,128)(2,1)} %mel.1, s32[1,32]{1,0:T(1,128)} %bitcast.4, s32[1,32]{1,0:T(1,128)} %bitcast.5, s32[1,32]{1,0:T(1,128)} %bitcast.6, s32[1,32]{1,0:T(1,128)} %bitcast.7, ...), custom_call_target="tpu_custom_call" | custom-call | tf_op jit(solution)/shard_map/pallas_call | solution.py:938
  201.2 0.0 copy-start.1
  201.2 1.8 copy.16
  203.0 0.0 copy-done.1
  203.0 0.0 copy-start
  203.0 0.7 copy.20
  203.7 0.4 copy-done
  204.1 0.0 copy-start.2
  204.1 0.7 copy.21
  204.8 0.0 copy-done.2
  204.8 0.6 copy.22
Async XLA Ops:
  201.2 1.9 copy-start.1
  203.0 1.1 copy-start
  204.1 0.7 copy-start.2

commit v5 on v4

--- a/solution.py
+++ b/solution.py
@@ -587,28 +587,28 @@
     both_parts = (0, 1)
     plan = {
         (0, 0): {
-            0: [(2, 4, (1,), 2), (1, 0, None, 2)],
-            1: [(2, 2, (1,), 1)],
-            2: [(2, 3, (0,), 1)],
-            3: [(2, 1, (0,), 0)],
+            0: [(2, 2, (0,), 1)],
+            1: [(2, 4, (1,), 2), (1, 0, None, 2)],
+            2: [(2, 2, (1,), 1)],
+            3: [(2, 3, (0,), 1)],
         },
         (0, 1): {
-            0: [(2, 3, (1,), 2), (1, 1, both_parts, 3)],
-            1: [(2, 1, (1,), 1)],
-            2: [(2, 4, (0,), 2), (1, 2, both_parts, 3)],
-            3: [(2, 2, (0,), 1)],
+            0: [(2, 1, (0,), 1)],
+            1: [(2, 3, (1,), 2), (1, 1, both_parts, 3)],
+            2: [(2, 1, (1,), 1)],
+            3: [(2, 4, (0,), 2), (1, 2, both_parts, 3)],
         },
         (1, 0): {
-            0: [(2, 1, (0,), 0)],
-            1: [(1, 1, both_parts, 1)],
-            2: [(2, 1, (1,), 0)],
-            3: [(1, 2, both_parts, 1)],
+            0: [],
+            1: [(2, 1, (0,), 0), (1, 1, both_parts, 1)],
+            2: [],
+            3: [(2, 1, (1,), 0), (1, 2, both_parts, 1)],
         },
         (1, 1): {
-            0: [(2, 2, (0,), 1)],
-            1: [(1, 3, both_parts, 2)],
-            2: [(2, 2, (1,), 1)],
-            3: [(1, 4, both_parts, 2), (1, 0, None, 1)],
+            0: [],
+            1: [(2, 2, (0,), 1), (1, 3, both_parts, 2)],
+            2: [],
+            3: [(2, 2, (1,), 1), (1, 4, both_parts, 2), (1, 0, None, 1)],
         },
     }
 
@@ -717,7 +717,7 @@
         rcopy(TT.at[2 * i + 1 - c], TS.at[i], tt_s.at[4, i], tt_r.at[4, i], sib).start()
 
     def tail(low, high, g):
-        done = 1 if g.cc == 0 else 2
+        done = 0 if g.cc == 0 else 2
         late = {0: 5, 2: 6, 3: 7} if g.cc == 0 and NX > 1 else {}
         for e in range(low, high):
             if late.get(e, 8) < 2 * g.h2:

time: 206 us -> 203 us (0.985)
  Pallas kernels: 199 us -> 196 us
    pallas_call x1, Pallas kernels: 199 us -> 196 us  [body(): pl.pallas_call(functools.partial(kernel, dims), out_shape=(jax.ShapeDtype...]
where the time goes in v5:
time: 203 us
  Pallas kernels  196 us (97%)
  local copies, waits for them, and re-layouts  5.84 us (3%)
    pallas_call x1, Pallas kernels, body(): pl.pallas_call(functools.partial(kernel, dims), out_shape=(jax.ShapeDtype...  196 us

profile of v5, /device:TPU:8, one launch (start us, length us, event | category | flops | bytes accessed | tf_op | source)
XLA Modules:
  0.0 202.7 jit_solution(11404962516959922662)
XLA Ops:
  0.6 1.6 copy.15.taps_in
  2.2 196.2 %shard_map.138 = (f32[1,48,1536]{2,1,0:T(8,128)}, f32[1,48,1536]{2,1,0:T(8,128)}, f32[1,31,1536]{2,1,0:T(8,128)}, f32[1,1536]{1,0:T(1,128)}) custom-call(bf16[32,4,320]{2,1,0:T(4,128)(2,1)} %mel.1, s32[1,32]{1,0:T(1,128)} %bitcast.4, s32[1,32]{1,0:T(1,128)} %bitcast.5, s32[1,32]{1,0:T(1,128)} %bitcast.6, s32[1,32]{1,0:T(1,128)} %bitcast.7, ...), custom_call_target="tpu_custom_call" | custom-call | tf_op jit(solution)/shard_map/pallas_call | solution.py:938
  198.5 0.0 copy-start.1
  198.5 1.8 copy.16
  200.3 0.0 copy-done.1
  200.3 0.0 copy-start
  200.3 0.7 copy.20
  201.0 0.4 copy-done
  201.4 0.0 copy-start.2
  201.4 0.7 copy.21
  202.1 0.0 copy-done.2
  202.1 0.6 copy.22
Async XLA Ops:
  198.5 1.9 copy-start.1
  200.3 1.1 copy-start
  201.4 0.7 copy-start.2

commit v6 on v5

--- a/solution.py
+++ b/solution.py
@@ -68,6 +68,7 @@
     CT,
     PF,
     XH,
+    ST,
     GO,
     GS,
     MS,
@@ -450,7 +451,9 @@
             for j, xx in xs_:
                 rcopy(X.at[s, x], X.at[s, xx], xf_s.at[s, j], xf_r.at[s, xx], dev(xx=xx)).wait()
 
-        _, shifted, inverse = statistics(s)
+        mean, shifted, inverse = statistics(s)
+        ST[s, 0] = jnp.broadcast_to(mean, (FRM, 128))
+        ST[s, 1] = jnp.broadcast_to(inverse, (FRM, 128))
         for b in range(NX):
             gain = GAIN[s % 2, s // 2, 0:1, b * DX : (b + 1) * DX]
             NT[s, :, b * DX : (b + 1) * DX] = (shifted[b] * inverse * gain).astype(BF16)
@@ -652,9 +655,10 @@
             rcopy(GO.at[s], GS.at[i], sg_s.at[i], sg_r.at[i], sib).start()
 
         pump_back(s, 0)
-        mean, shifted, inverse = statistics(s)
+        mean = jnp.concatenate([ST[s, 0]] * lanes_x, axis=1)
+        inverse = jnp.concatenate([ST[s, 1]] * lanes_x, axis=1)
         for b in range(NX):
-            XH[b] = shifted[b] * inverse
+            XH[b] = (X[s, b].astype(F32) - mean) * inverse
         sum_a = jnp.zeros((FRM, 1), F32)
         sum_b = jnp.zeros((FRM, 1), F32)
         per = NY // NX
@@ -880,6 +884,7 @@
         vm((FRM, DX), BF16),
         vm((FRM, DX)),
         vm((NX, FRM, DX)),
+        vm((SECT, 2, FRM, 128)),
         vm((SECT, FRM, 2 * DX), BF16),
         vm((NX, FRM, 2 * DX), BF16),
         vm((NX, FRM, DX), BF16),

time: 203 us -> 203 us (level)
  no operation moved by 1% of the time
where the time goes in v6:
time: 203 us
  Pallas kernels  196 us (97%)
  local copies, waits for them, and re-layouts  5.84 us (3%)
    pallas_call x1, Pallas kernels, body(): pl.pallas_call(functools.partial(kernel, dims), out_shape=(jax.ShapeDtype...  196 us

profile of v6, /device:TPU:8, one launch (start us, length us, event | category | flops | bytes accessed | tf_op | source)
XLA Modules:
  0.0 202.8 jit_solution(7484686325995295471)
XLA Ops:
  0.6 1.6 copy.15.taps_in
  2.2 196.3 %shard_map.138 = (f32[1,48,1536]{2,1,0:T(8,128)}, f32[1,48,1536]{2,1,0:T(8,128)}, f32[1,31,1536]{2,1,0:T(8,128)}, f32[1,1536]{1,0:T(1,128)}) custom-call(bf16[32,4,320]{2,1,0:T(4,128)(2,1)} %mel.1, s32[1,32]{1,0:T(1,128)} %bitcast.4, s32[1,32]{1,0:T(1,128)} %bitcast.5, s32[1,32]{1,0:T(1,128)} %bitcast.6, s32[1,32]{1,0:T(1,128)} %bitcast.7, ...), custom_call_target="tpu_custom_call" | custom-call | tf_op jit(solution)/shard_map/pallas_call | solution.py:943
  198.6 0.0 copy-start.1
  198.6 1.8 copy.16
  200.4 0.0 copy-done.1
  200.4 0.0 copy-start
  200.4 0.7 copy.20
  201.1 0.4 copy-done
  201.5 0.0 copy-start.2
  201.5 0.7 copy.21
  202.2 0.0 copy-done.2
  202.2 0.6 copy.22
Async XLA Ops:
  198.6 1.9 copy-start.1
  200.4 1.1 copy-start
  201.5 0.7 copy-start.2
